TPU v7x, 256 devices: a whole 4x4x8 slice. The times are simulated.
256 devices in a mesh: row: 8 (over z), col: 32 (over y, x, core).
Axes of the slice: x: 4, y: 4, z: 8, core: 2. Of those that a mesh axis runs over, the one named last changes fastest.
Arguments:
- activations: bfloat16 [262144, 1280], P(('row', 'col')), may hold values from -50 to 50
- out_grads: bfloat16 [262144, 1280], P(('row', 'col')), may hold values from -0.046875 to 0.046875
- error_buffer: bfloat16 [327680, 1280], P(('row', 'col')), may hold values from -8 to 8
- start_q: float32 [8, 1280], replicated, may hold values from -6 to 6
Outputs:
- new_error: bfloat16 [327680, 1280], P(('row', 'col'))
- factor_q: float32 [8, 1280], replicated
All inputs are finite; a program needn't handle non-finite values.
Results may differ from a plain program's by a relative error of at most 0.001.
Values sent between devices are 32-bit elements; how exact they have to be, the bound alone decides.
No kernel may reach another device: no remote copies, remote signals or barrier semaphores. Data moves between devices by JAX's collectives and lax.ppermute only.
A program may use at most 64 MiB of HBM per device.

v0:
```python
import jax
import jax.numpy as jnp
from jax import lax
from jax.sharding import PartitionSpec as P


def orthonormal(p_sum):
    highest = lax.Precision.HIGHEST
    done = []
    for index in range(p_sum.shape[0]):
        vector = p_sum[index]
        for basis in done:
            vector = vector - jnp.dot(basis, vector, precision=highest) * basis
        vector = vector / jnp.sqrt(jnp.dot(vector, vector, precision=highest))
        done.append(vector)
    return jnp.stack(done)


def on_device(activations, out_grads, error_buffer, start_q):
    highest = lax.Precision.HIGHEST
    replicas = lax.axis_size("row") * lax.axis_size("col")
    grad_part = lax.dot_general(
        activations, out_grads, (((0,), (0,)), ((), ())), preferred_element_type=jnp.float32
    )
    merged = grad_part + error_buffer.astype(jnp.float32)
    p_rows = lax.psum(
        lax.dot_general(start_q, merged, (((1,), (1,)), ((), ())), precision=highest), "row"
    )
    p_hat = orthonormal(lax.psum(p_rows, "col"))
    q_total = lax.psum(jnp.dot(p_hat, merged, precision=highest), ("row", "col"))
    factor_q = q_total / jnp.float32(replicas)
    update = lax.dot_general(p_hat, factor_q, (((0,), (0,)), ((), ())), precision=highest)
    return ((merged - update).astype(jnp.bfloat16), factor_q)


def solution(mesh):
    return jax.shard_map(
        on_device,
        mesh=mesh,
        in_specs=(P(("row", "col"), None), P(("row", "col"), None), P(("row", "col"), None), P()),
        out_specs=(P(("row", "col"), None), P()),
        check_vma=False,
    )
```

profile of v0, /device:TPU:1, one launch (start us, length us, event | category | flops | bytes accessed | tf_op | source)
XLA Modules:
  0.0 302.8 jit_solution(15548405272012858571)
XLA Ops:
  0.7 1.7 copy-done
  2.4 6.3 %convolution_add_fusion = f32[1280,1280]{1,0:T(8,128)S(1)} fusion(bf16[1024,1280]{1,0:T(8,128)(2,1)S(1)} %copy-done, bf16[1024,1280]{1,0:T(8,128)(2,1)} %param.5, bf16[1280,1280]{1,0:T(8,128)(2,1)} %param.6), kind=kOutput, calls=%fused_computation.1 | convolution fusion | flops 3358720000 | bytes 15073280 | tf_op jit(solution)/shard_map/dot_general | solution.py:22
  8.7 2.7 copy-done.1
  11.4 5.5 %convolution_bitcast_fusion = f32[8,1280]{1,0:T(8,128)S(1)} fusion(f32[1280,1280]{1,0:T(8,128)S(1)} %convolution_add_fusion, f32[8,1280]{1,0:T(8,128)S(1)} %copy-done.3), kind=kOutput, calls=%fused_computation.3 | convolution fusion | flops 157286400 | bytes 6635520 | tf_op jit(solution)/shard_map/dot_general | solution.py:27
  17.0 27.0 %psum.21 = f32[8,1280]{1,0:T(8,128)S(1)} all-reduce(f32[8,1280]{1,0:T(8,128)S(1)} %convolution_bitcast_fusion), channel_id=1, replica_groups=mesh['row'=8,'col'=32] {'row'}, use_global_device_ids=true, to_apply=%region_0.0 | all-reduce | flops 10240 | bytes 81920 | tf_op jit(solution)/shard_map/psum | solution.py:26
  43.9 126.3 %psum.22 = f32[8,1280]{1,0:T(8,128)S(1)} all-reduce(f32[8,1280]{1,0:T(8,128)S(1)} %psum.21), channel_id=1, replica_groups=mesh['row'=8,'col'=32] {'col'}, use_global_device_ids=true, to_apply=%region_1.0 | all-reduce | flops 10240 | bytes 81920 | tf_op jit(solution)/shard_map/psum | solution.py:29
  172.2 0.7 slice_reduce_fusion
  172.9 0.7 multiply_reduce_fusion.7
  174.3 4.5 %fusion.28 = (f32[1280]{0:T(1024)S(1)}, f32[1,1280]{1,0:T(1,128)S(1)}, f32[1280]{0:T(1024)S(1)}, f32[1,1280]{1,0:T(1,128)S(1)}, f32[1280]{0:T(1024)S(1)}, /*inde...) fusion(f32[1,1280]{1,0:T(1,128)S(1)} %get-tuple-element.92, ...), kind=kLoop, calls=%fused_computation.112 | loop fusion | flops 19200 | bytes 112672 | tf_op jit(solution)/shard_map/sub | solution.py:13
  178.8 0.7 multiply_reduce_fusion.6
  179.5 3.8 %fusion.10 = (f32[1280]{0:T(1024)S(1)}, f32[1280]{0:T(1024)S(1)}, f32[1280]{0:T(1024)S(1)}, f32[1280]{0:T(1024)S(1)}, f32[1280]{0:T(1024)S(1)}, /*index=5*/f32[1280]{0:T(1024)S(1)}) fusion(f32[1,1280]{1,0:T(1,128)S(1)} %get-tuple-element.94, f32[1,1280]{1,0:T(1,128)S(1)} %get-tuple-element.104, f32[]{:T(128)} %get-tuple-element.25, ...), kind=kLoop, calls=%fused_computation.94 | loop fusion | flops 15360 | bytes 66584 | tf_op jit(solution)/shard_map/sub | solution.py:13
  184.6 0.7 fusion.27
  185.3 0.7 multiply_reduce_fusion.5
  185.9 6.3 %fusion.21 = (f32[1280]{0:T(1024)S(1)}, f32[1,1280]{1,0:T(1,128)S(1)}, f32[1280]{0:T(1024)S(1)}, f32[1,1280]{1,0:T(1,128)S(1)}, f32[1280]{0:T(1024)S(1)}, /*inde...) fusion(f32[1,1280]{1,0:T(1,128)S(1)} %get-tuple-element.76, ...), kind=kLoop, calls=%fused_computation.105 | loop fusion | flops 25600 | bytes 87080 | tf_op jit(solution)/shard_map/sub | solution.py:13
  193.6 0.7 multiply_reduce_fusion.4
  194.3 2.6 fusion.11
  198.8 0.7 multiply_reduce_fusion.3
  199.4 3.8 %fusion.16 = (f32[1280]{0:T(1024)S(1)}, f32[1,1280]{1,0:T(1,128)S(1)}, f32[1280]{0:T(1024)S(1)}, f32[1,1280]{1,0:T(1,128)S(1)}, f32[1280]{0:T(1024)S(1)}, /*index=5*/f32[1,1280]{1,0:T(1,128)S(1)}) fusion(f32[1,1280]{1,0:T(1,128)S(1)} %get-tuple-element.62, f32[]{:T(128)} %get-tuple-element.14, f32[1,1280]{1,0:T(1,128)S(1)} %get-tuple-element.112, ...), kind=kLoop, calls=%fused_computation.100 | loop fusion | flops 15360 | bytes 56344 | tf_op jit(solution)/shard_map/sub | solution.py:13
  205.2 1.3 fusion.12
  207.8 0.7 fusion.15
  209.1 1.3 fusion.14
  211.8 5.9 %fusion.36 = f32[8,1280]{1,0:T(8,128)S(1)} fusion(f32[8,1280]{1,0:T(8,128)S(1)} %stack.2, f32[1280,1280]{1,0:T(8,128)} %copy-done.1), kind=kOutput, calls=%fused_computation.120 | convolution fusion | flops 157286400 | bytes 6635520 | tf_op jit(solution)/shard_map/dot_general | solution.py:30
  217.7 76.4 %psum.23 = f32[8,1280]{1,0:T(8,128)S(1)} all-reduce(f32[8,1280]{1,0:T(8,128)S(1)} %fusion.36), channel_id=1, replica_groups=mesh['row'=8,'col'=32] {'row','col'}, use_global_device_ids=true, to_apply=%region_2.0 | all-reduce | flops 10240 | bytes 81920 | tf_op jit(solution)/shard_map/psum | solution.py:30
  294.1 8.7 %fusion = bf16[1280,1280]{1,0:T(8,128)(2,1)} fusion(f32[1280,1280]{1,0:T(8,128)} %copy-done.1, f32[8,1280]{1,0:T(8,128)S(1)} %stack.2, f32[8,1280]{1,0:T(8,128)S(1)} %broadcast_multiply_fusion), kind=kOutput, calls=%fused_computation.2 | convolution fusion | flops 160563200 | bytes 9912320 | tf_op jit(solution)/shard_map/dot_general | solution.py:32
  (24 shorter events, 6.9 us)
Async XLA Ops:
  0.6 1.7 copy-start
  0.6 10.8 %copy-start.3 = (f32[8,1280]{1,0:T(8,128)S(1)}, f32[8,1280]{1,0:T(8,128)}, u32[]{:S(2)}) copy-start(f32[8,1280]{1,0:T(8,128)} %param.7) | copy-start | bytes 122884
  8.7 2.7 copy-start.1
  294.1 8.7 %copy-start.2 = (f32[8,1280]{1,0:T(8,128)}, f32[8,1280]{1,0:T(8,128)S(1)}, u32[]{:S(2)}) copy-start(f32[8,1280]{1,0:T(8,128)S(1)} %broadcast_multiply_fusion) | copy-start | bytes 122884
where the time goes:
time: 303 us
  blocking collectives  230 us (76%)
  other arithmetic  36 us (12%)
  matrix products  26.4 us (9%)
  between operations  6.2 us (2%)
  local copies, waits for them, and re-layouts  4.57 us (2%)
    psum x1, blocking collectives, on_device(): p_hat = orthonormal(lax.psum(p_rows, 'col'))  126 us
    psum x1, blocking collectives, on_device(): lax.psum(jnp.dot(p_hat, merged, precision=highest), ('row', 'col'))  76.4 us
    psum x1, blocking collectives, on_device(): lax.psum(lax.dot_general(start_q, merged, (((1,), (1,)), ((), ())), preci...  27 us
    sub x7, other arithmetic, orthonormal(): vector = vector - jnp.dot(basis, vector, precision=highest) * basis  23.7 us
    dot_general x1, matrix products, on_device(): lax.dot_general(p_hat, factor_q, (((0,), (0,)), ((), ())), precision=high...  8.68 us
    dot_general x1, matrix products, on_device(): lax.dot_general(activations, out_grads, (((0,), (0,)), ((), ())), preferr...  6.32 us

commit v1 on v0

v1 whole, which is shorter than its diff:
```python
import functools

import jax
import jax.numpy as jnp
from jax import lax
from jax.experimental import pallas as pl
from jax.experimental.pallas import tpu as pltpu
from jax.sharding import PartitionSpec as P

F32, BF16 = jnp.float32, jnp.bfloat16
BLOCK = 256
VMEM = pl.BlockSpec(memory_space=pltpu.VMEM)
ANY = pl.BlockSpec(memory_space=pl.ANY)
HBM = pl.BlockSpec(memory_space=pltpu.HBM)
AXES = ("row", "col")
NT = (((1,), (1,)), ((), ()))
NN = (((1,), (0,)), ((), ()))
TN = (((0,), (0,)), ((), ()))


def params():
    return pltpu.CompilerParams(vmem_limit_bytes=16 * 1024 * 1024)


def in_hbm(x):
    return pltpu.with_memory_space_constraint(x, pltpu.HBM)


def in_vmem(x):
    return pltpu.with_memory_space_constraint(x, pltpu.VMEM)


def parts_of(x):
    high = x.astype(BF16).astype(F32)
    rest = x - high
    mid = rest.astype(BF16).astype(F32)
    low = (rest - mid).astype(BF16).astype(F32)
    return high, mid, low


def stacked(x):
    high, mid, low = parts_of(x)
    return jnp.concatenate([high, mid, low, jnp.zeros_like(x)], axis=0).astype(BF16)


def times(lhs, rhs, dims):
    out = lax.dot_general(lhs, rhs, dims, preferred_element_type=F32)
    return out[0:8] + (out[8:16] + out[16:24])


def p_kernel(q_hbm, a_hbm, g_hbm, e_hbm, p_ref, a_ref, g_ref, e_ref, q_ref, sems, *, cuts):
    tokens, width = a_ref.shape
    copies = [pltpu.make_async_copy(q_hbm, q_ref, sems.at[0])]
    for src, dst, n in ((g_hbm, g_ref, cuts[0]), (a_hbm, a_ref, cuts[1]), (e_hbm, e_ref, cuts[2])):
        size = src.shape[0] // n
        for i in range(n):
            rows = pl.ds(i * size, size)
            copies.append(pltpu.make_async_copy(src.at[rows], dst.at[rows], sems.at[len(copies)]))
    for copy in copies:
        copy.start()
    queue = iter(copies)
    next(queue).wait()
    q = stacked(q_ref[...])
    lefts = []
    size = tokens // cuts[0]
    for i in range(cuts[0]):
        next(queue).wait()
        lefts.append(times(q, g_ref[pl.ds(i * size, size), :], NT))
    left = stacked(jnp.concatenate(lefts, axis=1))
    size = tokens // cuts[1]
    total = None
    for i in range(cuts[1]):
        next(queue).wait()
        at = slice(i * size, (i + 1) * size)
        term = times(left[:, at], a_ref[at, :], NN)
        total = term if total is None else total + term
    size = width // cuts[2]
    for i in range(cuts[2]):
        next(queue).wait()
        at = slice(i * size, (i + 1) * size)
        p_ref[:, at] = total[:, at] + times(q, e_ref[at, :], NT)


def p_local(start_q, activations, out_grads, error_buffer, cuts=(2, 2, 2)):
    return pl.pallas_call(
        functools.partial(p_kernel, cuts=cuts),
        out_shape=(
            jax.ShapeDtypeStruct(start_q.shape, F32),
            pltpu.VMEM(activations.shape, BF16),
            pltpu.VMEM(out_grads.shape, BF16),
            pltpu.VMEM(error_buffer.shape, BF16),
        ),
        in_specs=[HBM, HBM, HBM, HBM],
        out_specs=(VMEM, VMEM, VMEM, VMEM),
        scratch_shapes=[pltpu.VMEM(start_q.shape, F32), pltpu.SemaphoreType.DMA((1 + sum(cuts),))],
        compiler_params=params(),
        name="p_local",
    )(in_hbm(start_q), in_hbm(activations), in_hbm(out_grads), in_hbm(error_buffer))


def merged_rows(i, a_ref, g_ref, e_ref):
    at = slice(i * BLOCK, (i + 1) * BLOCK)
    product = lax.dot_general(a_ref[:, at], g_ref[...], TN, preferred_element_type=F32)
    return product + e_ref[at, :].astype(F32)


def merged_block(i, a, g, e, after):
    def kernel(a_ref, g_ref, e_ref, after_ref, m_ref):
        del after_ref
        m_ref[...] = merged_rows(i, a_ref, g_ref, e_ref)

    return pl.pallas_call(
        kernel,
        out_shape=pltpu.VMEM((BLOCK, e.shape[1]), F32),
        in_specs=[VMEM, VMEM, VMEM, ANY],
        out_specs=VMEM,
        compiler_params=params(),
        cost_estimate=pl.CostEstimate(
            flops=2 * a.shape[0] * BLOCK * g.shape[1], bytes_accessed=0, transcendentals=0
        ),
        name="merged_block",
    )(a, g, e, after)


def orthonormal(rest):
    rows = lax.broadcasted_iota(jnp.int32, (rest.shape[0], 1), 0)
    hat = jnp.zeros_like(rest)
    for j in range(rest.shape[0]):
        row = rest[j : j + 1]
        dots = jnp.sum(row * rest, axis=1, keepdims=True)
        square = dots[j : j + 1]
        hat = jnp.where(rows == j, row / jnp.sqrt(square), hat)
        rest = rest - (dots / square) * row
    return hat


def q_kernel(p_ref, a_ref, g_ref, e_ref, q_ref, hat_ref, m_ref, *, block):
    if block is not None:
        m_ref[...] = merged_rows(block, a_ref, g_ref, e_ref)
    hat = orthonormal(p_ref[...])
    hat_ref[...] = hat
    stack = stacked(hat)
    left = stacked(times(stack, a_ref[...], NT))
    q_ref[...] = times(stack, e_ref[...], NN) + times(left, g_ref[...], NN)


def q_local(p_sum, a, g, e, block):
    return pl.pallas_call(
        functools.partial(q_kernel, block=block),
        out_shape=(
            jax.ShapeDtypeStruct(p_sum.shape, F32),
            pltpu.VMEM(p_sum.shape, F32),
            pltpu.VMEM((BLOCK, e.shape[1]), F32),
        ),
        in_specs=[VMEM, VMEM, VMEM, VMEM],
        out_specs=(VMEM, VMEM, VMEM),
        compiler_params=params(),
        name="q_local",
    )(p_sum, a, g, e)


def update_kernel(total_ref, hat_ref, *refs, replicas, n):
    m_refs = refs[:n]
    out_hbm, f_hbm, f_ref, out_ref, sems = refs[n:]
    factor = total_ref[...] * (1.0 / replicas)
    f_ref[...] = factor
    copies = [pltpu.make_async_copy(f_ref, f_hbm, sems.at[n])]
    copies[0].start()
    p1, p2, p3 = parts_of(hat_ref[...])
    f1, f2, f3 = parts_of(factor)
    zero = jnp.zeros_like(p1)
    lhs = jnp.concatenate([p1, p1, p2, p2, p1, p3, zero, zero], axis=0).astype(BF16)
    rhs = jnp.concatenate([f1, f2, f1, f2, f3, f1, zero, zero], axis=0).astype(BF16)
    for i in range(n):
        at = slice(i * BLOCK, (i + 1) * BLOCK)
        update = lax.dot_general(lhs[:, at], rhs, TN, preferred_element_type=F32)
        out_ref[at, :] = (m_refs[i][...] - update).astype(BF16)
        copies.append(pltpu.make_async_copy(out_ref.at[at], out_hbm.at[at], sems.at[i]))
        copies[-1].start()
    for copy in copies:
        copy.wait()


def update(q_total, hat, blocks, replicas):
    n = len(blocks)
    shape = (n * BLOCK, q_total.shape[1])
    return pl.pallas_call(
        functools.partial(update_kernel, replicas=replicas, n=n),
        out_shape=(
            jax.ShapeDtypeStruct(shape, BF16),
            jax.ShapeDtypeStruct(q_total.shape, F32),
        ),
        in_specs=[VMEM] * (2 + n),
        out_specs=(HBM, HBM),
        scratch_shapes=[
            pltpu.VMEM(q_total.shape, F32),
            pltpu.VMEM(shape, BF16),
            pltpu.SemaphoreType.DMA((n + 1,)),
        ],
        compiler_params=params(),
        name="update",
    )(q_total, hat, *blocks)


CORES = 2


def permute(x, target):
    n_row, n_col = lax.axis_size("row"), lax.axis_size("col")
    pairs = []
    for i in range(n_row * n_col):
        row, col = target(*divmod(i, n_col))
        pairs.append((i, (row % n_row) * n_col + col))
    return lax.ppermute(x, AXES, pairs)


def gather_sum(x, groups):
    n = len(groups[0])
    every = jnp.broadcast_to(x[None], (n,) + x.shape)
    every = lax.all_to_all(every, AXES, 0, 0, axis_index_groups=groups, tiled=True)
    terms = [every[i] for i in range(n)]
    while len(terms) > 1:
        terms = [low + high for low, high in zip(terms[0::2], terms[1::2])]
    return terms[0]


def core_scatter(x, core, beside):
    half = x.shape[0] // CORES
    low, high = x[:half], x[half:]
    sent = jnp.where(core == 0, high, low)
    other, extra = lax.optimization_barrier((permute(sent, lambda r, c: (r, c ^ 1)), beside(sent)))
    return jnp.where(core == 0, low, high) + other, extra


def core_gather(x, core, beside):
    other, extra = lax.optimization_barrier((permute(x, lambda r, c: (r, c ^ 1)), beside(x)))
    rows = [jnp.where(core == 0, x, other), jnp.where(core == 0, other, x)]
    return jnp.concatenate(rows, axis=0), extra


def xy_groups():
    n_row, n_col = lax.axis_size("row"), lax.axis_size("col")
    return [
        [r * n_col + i * CORES + k for i in range(n_col // CORES)]
        for r in range(n_row)
        for k in range(CORES)
    ]


def z_groups():
    n_row, n_col = lax.axis_size("row"), lax.axis_size("col")
    return [[r * n_col + c for r in range(n_row)] for c in range(n_col)]


def on_device(activations, out_grads, error_buffer, start_q):
    replicas = lax.axis_size("row") * lax.axis_size("col")
    core = lax.axis_index("col") % CORES
    p, a, g, e = p_local(start_q, activations, out_grads, error_buffer)
    block = lambda i: lambda after: merged_block(i, a, g, e, after)
    p, m0 = core_scatter(p, core, block(0))
    p = gather_sum(gather_sum(p, xy_groups()), z_groups())
    p_sum, m1 = core_gather(p, core, block(1))
    q, hat, m2 = q_local(p_sum, a, g, e, 2)
    q, m3 = core_scatter(q, core, block(3))
    q = gather_sum(gather_sum(q, xy_groups()), z_groups())
    q_total, m4 = core_gather(q, core, block(4))
    return update(q_total, hat, [m0, m1, m2, m3, m4], replicas)


def solution(mesh):
    return jax.shard_map(
        on_device,
        mesh=mesh,
        in_specs=(P(AXES, None), P(AXES, None), P(AXES, None), P()),
        out_specs=(P(AXES, None), P()),
        check_vma=False,
    )
```

time: 303 us -> 75.9 us (0.25)
  blocking collectives: 230 us -> 52.1 us
  other arithmetic: 36 us -> 0.23 us
  matrix products: 26.4 us -> 0 us
  Pallas kernels: 0 us -> 12.9 us
  starting transfers between devices: 0 us -> 9.35 us
  between operations: 6.2 us -> 0.82 us
  local copies, waits for them, and re-layouts: 4.57 us -> 0.13 us
    psum x3 -> x0, blocking collectives: 230 us -> none  [the longest x1 126 us: on_device(): p_hat = orthonormal(lax.psum(p_rows, 'col'))]
    all_to_all x0 -> x4, blocking collectives: none -> 52.1 us  [gather_sum(): lax.all_to_all(every, AXES, 0, 0, axis_index_groups=groups, tiled=True)]
    dot_general x4 -> x0, matrix products: 26.4 us -> none  [the longest x1 8.68 us: on_device(): lax.dot_general(p_hat, factor_q, (((0,), (0,)), ((), ())), precision=high...]
    sub x7 -> x0, other arithmetic: 23.7 us -> none  [orthonormal(): vector = vector - jnp.dot(basis, vector, precision=highest) * basis]
    pallas_call x0 -> x7, Pallas kernels: none -> 12.9 us  [the longest x1 4.45 us: p_local(): pl.pallas_call(functools.partial(p_kernel, cuts=cuts), out_shape=(jax.Sha...]
    dot_general x15 -> x0, other arithmetic: 9.44 us -> none  [the longest x8 5.19 us: orthonormal(): vector = vector - jnp.dot(basis, vector, precision=highest) * basis]
    ppermute x0 -> x4, starting transfers between devices: none -> 9.35 us  [permute(): return lax.ppermute(x, AXES, pairs)]
    unnamed x8 -> x0, local copies, waits for them, and re-layouts: 4.46 us -> none
  transfers between devices with their start and end apart: 0 -> 4, of which waited for: 0 -> 0; matrix products, arithmetic and copies ran while one was open for 0% -> 0% of each run, Pallas kernels for 0% -> 5%
where the time goes in v1:
time: 75.9 us; the launch traced here: 75.6 us
  blocking collectives  52.1 us (69%)
  Pallas kernels  12.9 us (17%)
  starting transfers between devices  9.35 us (12%)
  between operations  0.82 us (1%)
    all_to_all x4, blocking collectives, gather_sum(): lax.all_to_all(every, AXES, 0, 0, axis_index_groups=groups, tiled=True)  52.1 us
    ppermute x4, starting transfers between devices, permute(): return lax.ppermute(x, AXES, pairs)  9.35 us
    pallas_call x1, Pallas kernels, p_local(): pl.pallas_call(functools.partial(p_kernel, cuts=cuts), out_shape=(jax.Sha...  4.45 us
    pallas_call x4, Pallas kernels, merged_block(): pl.pallas_call(kernel, out_shape=pltpu.VMEM((BLOCK, e.shape[1]), F32), in...  3.59 us
    pallas_call x1, Pallas kernels, q_local(): pl.pallas_call(functools.partial(q_kernel, block=block), out_shape=(jax.S...  2.79 us
    pallas_call x1, Pallas kernels, update(): pl.pallas_call(functools.partial(update_kernel, replicas=replicas, n=n),...  2.11 us
  transfers between devices with their start and end apart: 4, of which 0 were waited for; matrix products, arithmetic and copies ran while one was open for 0% of the time, Pallas kernels for 5%

profile of v1, /device:TPU:1, one launch (start us, length us, event | category | flops | bytes accessed | tf_op | source)
XLA Modules:
  0.0 75.6 jit_solution(11407493059207313678)
XLA Ops:
  0.6 4.4 %p_local.1 = (f32[8,1280]{1,0:T(8,128)S(1)}, bf16[1024,1280]{1,0:T(8,128)(2,1)S(1)}, bf16[1024,1280]{1,0:T(8,128)(2,1)S(1)}, bf16[1280,1280]{1,0:T(8,128)(2,1)S(1)}) custom-call(f32[8,1280]{1,0:T(8,128)} %q_hbm.1, bf16[1024,1280]{1,0:T(8,128)(2,1)} %a_hbm.1, bf16[1024,1280]{1,0:T(8,128)(2,1)} %g_hbm.1, bf16[1280,1280]{1,0:T(8,128)(2,1)} %e_hbm.1), custom_call_target="tpu_custom_call" | custom-call | tf_op jit(solution)/shard_map/p_local/pallas_call | solution.py:85
  5.1 3.3 %collective-permute-start = (f32[4,1280]{1,0:T(4,128)S(1)}, f32[4,1280]{1,0:T(4,128)S(1)}, u32[]{:S(2)}, u32[]{:S(2)}) collective-permute-start(f32[4,1280]{1,0:T(4,128)S(1)} %slice_select_fusion.1.after_ref), channel_id=1, source_target_pairs={{0,1},{1,0},{2,3},{3,2},{4,5},{5,4},{6,7},{7,6},{8,9},{9,8},{10,11... | collective-permute-start | bytes 61448 | tf_op jit(solution)/shard_map/ppermute | solution.py:214
  8.4 0.9 %merged_block.4.refs_0_ = f32[256,1280]{1,0:T(8,128)S(1)} custom-call(bf16[1024,1280]{1,0:T(8,128)(2,1)S(1)} %get-tuple-element.18.a_ref, bf16[1024,1280]{1,0:T(8,128)(2,1)S(1)} %get-tuple-element.19.g_ref, bf16[1280,1280]{1,0:T(8,128)(2,1)S(1)} %get-tuple-element.20.e_ref, f32[4,1280]{1,0:T(4,128)S(1)} %slice_select_fusion.1.after_ref), custom_call_target="tpu_custom_call" | custom-call | flops 671088640 | tf_op jit(solution)/shard_map/merged_block/pallas_call | solution.py:112
  9.3 0.0 collective-permute-done
  9.4 13.8 %all_to_all.20 = f32[16,4,1280]{2,1,0:T(4,128)S(1)} all-to-all(f32[16,4,1280]{2,1,0:T(4,128)S(1)} %broadcast_in_dim.12), channel_id=1, replica_groups={{0,2,4,6,8,10,12,14,16,18,20,22,24,26,28,30},{1,3,5,7,9,11,13,15,17,19,..., dimensions={0} | all-to-all | bytes 655360 | tf_op jit(solution)/shard_map/all_to_all | solution.py:220
  23.2 16.4 %all_to_all.21 = f32[8,4,1280]{2,1,0:T(4,128)S(1)} all-to-all(f32[8,4,1280]{2,1,0:T(4,128)S(1)} %broadcast_in_dim.14), channel_id=1, replica_groups={{0,32,64,96,128,160,192,224},{1,33,65,97,129,161,193,225},{2,34,66,98,1..., dimensions={0} | all-to-all | bytes 327680 | tf_op jit(solution)/shard_map/all_to_all | solution.py:220
  39.6 2.8 %collective-permute-start.1 = (f32[4,1280]{1,0:T(4,128)S(1)}, f32[4,1280]{1,0:T(4,128)S(1)}, u32[]{:S(2)}, u32[]{:S(2)}) collective-permute-start(f32[4,1280]{1,0:T(4,128)S(1)} %fusion.14.after_ref), channel_id=1, source_target_pairs={{0,1},{1,0},{2,3},{3,2},{4,5},{5,4},{6,7},{7,6},{8,9},{9,8},{10,11... | collective-permute-start | bytes 61448 | tf_op jit(solution)/shard_map/ppermute | solution.py:214
  42.5 0.9 %merged_block.5.refs_1_ = f32[256,1280]{1,0:T(8,128)S(1)} custom-call(bf16[1024,1280]{1,0:T(8,128)(2,1)S(1)} %get-tuple-element.18.a_ref, bf16[1024,1280]{1,0:T(8,128)(2,1)S(1)} %get-tuple-element.19.g_ref, bf16[1280,1280]{1,0:T(8,128)(2,1)S(1)} %get-tuple-element.20.e_ref, f32[4,1280]{1,0:T(4,128)S(1)} %fusion.14.after_ref), custom_call_target="tpu_custom_call" | custom-call | flops 671088640 | tf_op jit(solution)/shard_map/merged_block/pallas_call | solution.py:112
  43.4 0.0 collective-permute-done.1
  43.4 2.8 %q_local.1 = (f32[8,1280]{1,0:T(8,128)S(1)}, f32[8,1280]{1,0:T(8,128)S(1)}, f32[256,1280]{1,0:T(8,128)S(1)}) custom-call(f32[8,1280]{1,0:T(8,128)S(1)} %pad_maximum_fusion.p_ref, bf16[1024,1280]{1,0:T(8,128)(2,1)S(1)} %get-tuple-element.18.a_ref, bf16[1024,1280]{1,0:T(8,128)(2,1)S(1)} %get-tuple-element.19.g_ref, bf16[1280,1280]{1,0:T(8,128)(2,1)S(1)} %get-tuple-element.20.e_ref), custom_call_target="tpu_custom_call" | custom-call | tf_op jit(solution)/shard_map/q_local/pallas_call | solution.py:148
  46.2 0.4 collective-permute-start.2
  46.6 0.9 %merged_block.6.refs_3_ = f32[256,1280]{1,0:T(8,128)S(1)} custom-call(bf16[1024,1280]{1,0:T(8,128)(2,1)S(1)} %get-tuple-element.18.a_ref, bf16[1024,1280]{1,0:T(8,128)(2,1)S(1)} %get-tuple-element.19.g_ref, bf16[1280,1280]{1,0:T(8,128)(2,1)S(1)} %get-tuple-element.20.e_ref, f32[4,1280]{1,0:T(4,128)S(1)} %slice_select_fusion.after_ref), custom_call_target="tpu_custom_call" | custom-call | flops 671088640 | tf_op jit(solution)/shard_map/merged_block/pallas_call | solution.py:112
  47.5 0.0 collective-permute-done.2
  47.6 11.6 %all_to_all.22 = f32[16,4,1280]{2,1,0:T(4,128)S(1)} all-to-all(f32[16,4,1280]{2,1,0:T(4,128)S(1)} %broadcast_in_dim.15), channel_id=1, replica_groups={{0,2,4,6,8,10,12,14,16,18,20,22,24,26,28,30},{1,3,5,7,9,11,13,15,17,19,..., dimensions={0} | all-to-all | bytes 655360 | tf_op jit(solution)/shard_map/all_to_all | solution.py:220
  59.2 10.5 %all_to_all.23 = f32[8,4,1280]{2,1,0:T(4,128)S(1)} all-to-all(f32[8,4,1280]{2,1,0:T(4,128)S(1)} %broadcast_in_dim.33), channel_id=1, replica_groups={{0,32,64,96,128,160,192,224},{1,33,65,97,129,161,193,225},{2,34,66,98,1..., dimensions={0} | all-to-all | bytes 327680 | tf_op jit(solution)/shard_map/all_to_all | solution.py:220
  69.7 2.8 %collective-permute-start.3 = (f32[4,1280]{1,0:T(4,128)S(1)}, f32[4,1280]{1,0:T(4,128)S(1)}, u32[]{:S(2)}, u32[]{:S(2)}) collective-permute-start(f32[4,1280]{1,0:T(4,128)S(1)} %fusion.2.after_ref), channel_id=1, source_target_pairs={{0,1},{1,0},{2,3},{3,2},{4,5},{5,4},{6,7},{7,6},{8,9},{9,8},{10,11... | collective-permute-start | bytes 61448 | tf_op jit(solution)/shard_map/ppermute | solution.py:214
  72.5 0.9 %merged_block.7.refs_4_ = f32[256,1280]{1,0:T(8,128)S(1)} custom-call(bf16[1024,1280]{1,0:T(8,128)(2,1)S(1)} %get-tuple-element.18.a_ref, bf16[1024,1280]{1,0:T(8,128)(2,1)S(1)} %get-tuple-element.19.g_ref, bf16[1280,1280]{1,0:T(8,128)(2,1)S(1)} %get-tuple-element.20.e_ref, f32[4,1280]{1,0:T(4,128)S(1)} %fusion.2.after_ref), custom_call_target="tpu_custom_call" | custom-call | flops 671088640 | tf_op jit(solution)/shard_map/merged_block/pallas_call | solution.py:112
  73.4 0.0 collective-permute-done.3
  73.5 2.1 %update.1 = (bf16[1280,1280]{1,0:T(8,128)(2,1)}, f32[8,1280]{1,0:T(8,128)}) custom-call(f32[8,1280]{1,0:T(8,128)S(1)} %pad_maximum_fusion.1.total_ref, f32[8,1280]{1,0:T(8,128)S(1)} %get-tuple-element.26.hat_ref, f32[256,1280]{1,0:T(8,128)S(1)} %merged_block.4.refs_0_, f32[256,1280]{1,0:T(8,128)S(1)} %merged_block.5.refs_1_, ...), custom_call_target="tpu_custom_call" | custom-call | tf_op jit(solution)/shard_map/update/pallas_call | solution.py:187
  (16 shorter events, 0.4 us)
Async XLA Ops:
  5.1 4.2 %collective-permute-start = (f32[4,1280]{1,0:T(4,128)S(1)}, f32[4,1280]{1,0:T(4,128)S(1)}, u32[]{:S(2)}, u32[]{:S(2)}) collective-permute-start(f32[4,1280]{1,0:T(4,128)S(1)} %slice_select_fusion.1.after_ref), channel_id=1, source_target_pairs={{0,1},{1,0},{2,3},{3,2},{4,5},{5,4},{6,7},{7,6},{8,9},{9,8},{10,11... | collective-permute-start | bytes 61448 | tf_op jit(solution)/shard_map/ppermute | solution.py:214
  39.6 3.7 %collective-permute-start.1 = (f32[4,1280]{1,0:T(4,128)S(1)}, f32[4,1280]{1,0:T(4,128)S(1)}, u32[]{:S(2)}, u32[]{:S(2)}) collective-permute-start(f32[4,1280]{1,0:T(4,128)S(1)} %fusion.14.after_ref), channel_id=1, source_target_pairs={{0,1},{1,0},{2,3},{3,2},{4,5},{5,4},{6,7},{7,6},{8,9},{9,8},{10,11... | collective-permute-start | bytes 61448 | tf_op jit(solution)/shard_map/ppermute | solution.py:214
  46.2 1.3 %collective-permute-start.2 = (f32[4,1280]{1,0:T(4,128)S(1)}, f32[4,1280]{1,0:T(4,128)S(1)}, u32[]{:S(2)}, u32[]{:S(2)}) collective-permute-start(f32[4,1280]{1,0:T(4,128)S(1)} %slice_select_fusion.after_ref), channel_id=1, source_target_pairs={{0,1},{1,0},{2,3},{3,2},{4,5},{5,4},{6,7},{7,6},{8,9},{9,8},{10,11... | collective-permute-start | bytes 61448 | tf_op jit(solution)/shard_map/ppermute | solution.py:214
  69.7 3.7 %collective-permute-start.3 = (f32[4,1280]{1,0:T(4,128)S(1)}, f32[4,1280]{1,0:T(4,128)S(1)}, u32[]{:S(2)}, u32[]{:S(2)}) collective-permute-start(f32[4,1280]{1,0:T(4,128)S(1)} %fusion.2.after_ref), channel_id=1, source_target_pairs={{0,1},{1,0},{2,3},{3,2},{4,5},{5,4},{6,7},{7,6},{8,9},{9,8},{10,11... | collective-permute-start | bytes 61448 | tf_op jit(solution)/shard_map/ppermute | solution.py:214

commit v2 on v1

--- a/solution.py
+++ b/solution.py
@@ -238,31 +238,32 @@
     return jnp.concatenate(rows, axis=0), extra
 
 
-def xy_groups():
+def xy_groups(step):
     n_row, n_col = lax.axis_size("row"), lax.axis_size("col")
+    n = n_col // CORES
     return [
-        [r * n_col + i * CORES + k for i in range(n_col // CORES)]
+        [r * n_col + i * step % n * CORES + k for i in range(n)]
         for r in range(n_row)
         for k in range(CORES)
     ]
 
 
-def z_groups():
-    n_row, n_col = lax.axis_size("row"), lax.axis_size("col")
-    return [[r * n_col + c for r in range(n_row)] for c in range(n_col)]
+def z_groups(order):
+    n_col = lax.axis_size("col")
+    return [[r * n_col + c for r in order] for c in range(n_col)]
 
 
 def on_device(activations, out_grads, error_buffer, start_q):
     replicas = lax.axis_size("row") * lax.axis_size("col")
-    core = lax.axis_index("col") % CORES
+    core = lax.axis_index("col") & (CORES - 1)
     p, a, g, e = p_local(start_q, activations, out_grads, error_buffer)
     block = lambda i: lambda after: merged_block(i, a, g, e, after)
     p, m0 = core_scatter(p, core, block(0))
-    p = gather_sum(gather_sum(p, xy_groups()), z_groups())
+    p = gather_sum(gather_sum(p, xy_groups(7)), z_groups([1, 2, 0, 7, 6, 3, 5, 4]))
     p_sum, m1 = core_gather(p, core, block(1))
     q, hat, m2 = q_local(p_sum, a, g, e, 2)
     q, m3 = core_scatter(q, core, block(3))
-    q = gather_sum(gather_sum(q, xy_groups()), z_groups())
+    q = gather_sum(gather_sum(q, xy_groups(1)), z_groups([1, 2, 0, 7, 6, 3, 5, 4]))
     q_total, m4 = core_gather(q, core, block(4))
     return update(q_total, hat, [m0, m1, m2, m3, m4], replicas)
 

time: 75.9 us -> 74.6 us (0.983)
  blocking collectives: 52.1 us -> 50.8 us
    all_to_all x4, blocking collectives: 52.1 us -> 50.8 us  [gather_sum(): lax.all_to_all(every, AXES, 0, 0, axis_index_groups=groups, tiled=True)]
where the time goes in v2:
time: 74.6 us; the launch traced here: 74.4 us
  blocking collectives  50.8 us (68%)
  Pallas kernels  12.9 us (17%)
  starting transfers between devices  9.41 us (13%)
  between operations  0.81 us (1%)
    all_to_all x4, blocking collectives, gather_sum(): lax.all_to_all(every, AXES, 0, 0, axis_index_groups=groups, tiled=True)  50.8 us
    ppermute x4, starting transfers between devices, permute(): return lax.ppermute(x, AXES, pairs)  9.41 us
    pallas_call x1, Pallas kernels, p_local(): pl.pallas_call(functools.partial(p_kernel, cuts=cuts), out_shape=(jax.Sha...  4.44 us
    pallas_call x4, Pallas kernels, merged_block(): pl.pallas_call(kernel, out_shape=pltpu.VMEM((BLOCK, e.shape[1]), F32), in...  3.6 us
    pallas_call x1, Pallas kernels, q_local(): pl.pallas_call(functools.partial(q_kernel, block=block), out_shape=(jax.S...  2.79 us
    pallas_call x1, Pallas kernels, update(): pl.pallas_call(functools.partial(update_kernel, replicas=replicas, n=n),...  2.11 us
  transfers between devices with their start and end apart: 4, of which 0 were waited for; matrix products, arithmetic and copies ran while one was open for 0% of the time, Pallas kernels for 5%

profile of v2, /device:TPU:1, one launch (start us, length us, event | category | flops | bytes accessed | tf_op | source)
XLA Modules:
  0.0 74.4 jit_solution(4431957828594788283)
XLA Ops:
  0.6 4.4 %p_local.1 = (f32[8,1280]{1,0:T(8,128)S(1)}, bf16[1024,1280]{1,0:T(8,128)(2,1)S(1)}, bf16[1024,1280]{1,0:T(8,128)(2,1)S(1)}, bf16[1280,1280]{1,0:T(8,128)(2,1)S(1)}) custom-call(f32[8,1280]{1,0:T(8,128)} %q_hbm.1, bf16[1024,1280]{1,0:T(8,128)(2,1)} %a_hbm.1, bf16[1024,1280]{1,0:T(8,128)(2,1)} %g_hbm.1, bf16[1280,1280]{1,0:T(8,128)(2,1)} %e_hbm.1), custom_call_target="tpu_custom_call" | custom-call | tf_op jit(solution)/shard_map/p_local/pallas_call | solution.py:85
  5.1 3.3 %collective-permute-start = (f32[4,1280]{1,0:T(4,128)S(1)}, f32[4,1280]{1,0:T(4,128)S(1)}, u32[]{:S(2)}, u32[]{:S(2)}) collective-permute-start(f32[4,1280]{1,0:T(4,128)S(1)} %slice_select_fusion.1.after_ref), channel_id=1, source_target_pairs={{0,1},{1,0},{2,3},{3,2},{4,5},{5,4},{6,7},{7,6},{8,9},{9,8},{10,11... | collective-permute-start | bytes 61448 | tf_op jit(solution)/shard_map/ppermute | solution.py:214
  8.4 0.9 %merged_block.4.refs_0_ = f32[256,1280]{1,0:T(8,128)S(1)} custom-call(bf16[1024,1280]{1,0:T(8,128)(2,1)S(1)} %get-tuple-element.18.a_ref, bf16[1024,1280]{1,0:T(8,128)(2,1)S(1)} %get-tuple-element.19.g_ref, bf16[1280,1280]{1,0:T(8,128)(2,1)S(1)} %get-tuple-element.20.e_ref, f32[4,1280]{1,0:T(4,128)S(1)} %slice_select_fusion.1.after_ref), custom_call_target="tpu_custom_call" | custom-call | flops 671088640 | tf_op jit(solution)/shard_map/merged_block/pallas_call | solution.py:112
  9.3 0.0 collective-permute-done
  9.4 12.6 %all_to_all.20 = f32[16,4,1280]{2,1,0:T(4,128)S(1)} all-to-all(f32[16,4,1280]{2,1,0:T(4,128)S(1)} %broadcast_in_dim.12), channel_id=1, replica_groups={{0,14,28,10,24,6,20,2,16,30,12,26,8,22,4,18},{1,15,29,11,25,7,21,3,17,3..., dimensions={0} | all-to-all | bytes 655360 | tf_op jit(solution)/shard_map/all_to_all | solution.py:220
  22.1 15.4 %all_to_all.21 = f32[8,4,1280]{2,1,0:T(4,128)S(1)} all-to-all(f32[8,4,1280]{2,1,0:T(4,128)S(1)} %broadcast_in_dim.14), channel_id=1, replica_groups={{32,64,0,224,192,96,160,128},{33,65,1,225,193,97,161,129},{34,66,2,226,..., dimensions={0} | all-to-all | bytes 327680 | tf_op jit(solution)/shard_map/all_to_all | solution.py:220
  37.5 3.0 %collective-permute-start.1 = (f32[4,1280]{1,0:T(4,128)S(1)}, f32[4,1280]{1,0:T(4,128)S(1)}, u32[]{:S(2)}, u32[]{:S(2)}) collective-permute-start(f32[4,1280]{1,0:T(4,128)S(1)} %fusion.14.after_ref), channel_id=1, source_target_pairs={{0,1},{1,0},{2,3},{3,2},{4,5},{5,4},{6,7},{7,6},{8,9},{9,8},{10,11... | collective-permute-start | bytes 61448 | tf_op jit(solution)/shard_map/ppermute | solution.py:214
  40.6 0.9 %merged_block.5.refs_1_ = f32[256,1280]{1,0:T(8,128)S(1)} custom-call(bf16[1024,1280]{1,0:T(8,128)(2,1)S(1)} %get-tuple-element.18.a_ref, bf16[1024,1280]{1,0:T(8,128)(2,1)S(1)} %get-tuple-element.19.g_ref, bf16[1280,1280]{1,0:T(8,128)(2,1)S(1)} %get-tuple-element.20.e_ref, f32[4,1280]{1,0:T(4,128)S(1)} %fusion.14.after_ref), custom_call_target="tpu_custom_call" | custom-call | flops 671088640 | tf_op jit(solution)/shard_map/merged_block/pallas_call | solution.py:112
  41.5 0.0 collective-permute-done.1
  41.5 2.8 %q_local.1 = (f32[8,1280]{1,0:T(8,128)S(1)}, f32[8,1280]{1,0:T(8,128)S(1)}, f32[256,1280]{1,0:T(8,128)S(1)}) custom-call(f32[8,1280]{1,0:T(8,128)S(1)} %pad_maximum_fusion.p_ref, bf16[1024,1280]{1,0:T(8,128)(2,1)S(1)} %get-tuple-element.18.a_ref, bf16[1024,1280]{1,0:T(8,128)(2,1)S(1)} %get-tuple-element.19.g_ref, bf16[1280,1280]{1,0:T(8,128)(2,1)S(1)} %get-tuple-element.20.e_ref), custom_call_target="tpu_custom_call" | custom-call | tf_op jit(solution)/shard_map/q_local/pallas_call | solution.py:148
  44.3 0.4 collective-permute-start.2
  44.7 0.9 %merged_block.6.refs_3_ = f32[256,1280]{1,0:T(8,128)S(1)} custom-call(bf16[1024,1280]{1,0:T(8,128)(2,1)S(1)} %get-tuple-element.18.a_ref, bf16[1024,1280]{1,0:T(8,128)(2,1)S(1)} %get-tuple-element.19.g_ref, bf16[1280,1280]{1,0:T(8,128)(2,1)S(1)} %get-tuple-element.20.e_ref, f32[4,1280]{1,0:T(4,128)S(1)} %slice_select_fusion.after_ref), custom_call_target="tpu_custom_call" | custom-call | flops 671088640 | tf_op jit(solution)/shard_map/merged_block/pallas_call | solution.py:112
  45.6 0.0 collective-permute-done.2
  45.7 12.9 %all_to_all.22 = f32[16,4,1280]{2,1,0:T(4,128)S(1)} all-to-all(f32[16,4,1280]{2,1,0:T(4,128)S(1)} %broadcast_in_dim.15), channel_id=1, replica_groups={{0,2,4,6,8,10,12,14,16,18,20,22,24,26,28,30},{1,3,5,7,9,11,13,15,17,19,..., dimensions={0} | all-to-all | bytes 655360 | tf_op jit(solution)/shard_map/all_to_all | solution.py:220
  58.7 9.9 %all_to_all.23 = f32[8,4,1280]{2,1,0:T(4,128)S(1)} all-to-all(f32[8,4,1280]{2,1,0:T(4,128)S(1)} %broadcast_in_dim.33), channel_id=1, replica_groups={{32,64,0,224,192,96,160,128},{33,65,1,225,193,97,161,129},{34,66,2,226,..., dimensions={0} | all-to-all | bytes 327680 | tf_op jit(solution)/shard_map/all_to_all | solution.py:220
  68.6 2.7 %collective-permute-start.3 = (f32[4,1280]{1,0:T(4,128)S(1)}, f32[4,1280]{1,0:T(4,128)S(1)}, u32[]{:S(2)}, u32[]{:S(2)}) collective-permute-start(f32[4,1280]{1,0:T(4,128)S(1)} %fusion.2.after_ref), channel_id=1, source_target_pairs={{0,1},{1,0},{2,3},{3,2},{4,5},{5,4},{6,7},{7,6},{8,9},{9,8},{10,11... | collective-permute-start | bytes 61448 | tf_op jit(solution)/shard_map/ppermute | solution.py:214
  71.3 0.9 %merged_block.7.refs_4_ = f32[256,1280]{1,0:T(8,128)S(1)} custom-call(bf16[1024,1280]{1,0:T(8,128)(2,1)S(1)} %get-tuple-element.18.a_ref, bf16[1024,1280]{1,0:T(8,128)(2,1)S(1)} %get-tuple-element.19.g_ref, bf16[1280,1280]{1,0:T(8,128)(2,1)S(1)} %get-tuple-element.20.e_ref, f32[4,1280]{1,0:T(4,128)S(1)} %fusion.2.after_ref), custom_call_target="tpu_custom_call" | custom-call | flops 671088640 | tf_op jit(solution)/shard_map/merged_block/pallas_call | solution.py:112
  72.2 0.0 collective-permute-done.3
  72.2 2.1 %update.1 = (bf16[1280,1280]{1,0:T(8,128)(2,1)}, f32[8,1280]{1,0:T(8,128)}) custom-call(f32[8,1280]{1,0:T(8,128)S(1)} %pad_maximum_fusion.1.total_ref, f32[8,1280]{1,0:T(8,128)S(1)} %get-tuple-element.26.hat_ref, f32[256,1280]{1,0:T(8,128)S(1)} %merged_block.4.refs_0_, f32[256,1280]{1,0:T(8,128)S(1)} %merged_block.5.refs_1_, ...), custom_call_target="tpu_custom_call" | custom-call | tf_op jit(solution)/shard_map/update/pallas_call | solution.py:187
  (16 shorter events, 0.4 us)
Async XLA Ops:
  5.1 4.2 %collective-permute-start = (f32[4,1280]{1,0:T(4,128)S(1)}, f32[4,1280]{1,0:T(4,128)S(1)}, u32[]{:S(2)}, u32[]{:S(2)}) collective-permute-start(f32[4,1280]{1,0:T(4,128)S(1)} %slice_select_fusion.1.after_ref), channel_id=1, source_target_pairs={{0,1},{1,0},{2,3},{3,2},{4,5},{5,4},{6,7},{7,6},{8,9},{9,8},{10,11... | collective-permute-start | bytes 61448 | tf_op jit(solution)/shard_map/ppermute | solution.py:214
  37.5 3.9 %collective-permute-start.1 = (f32[4,1280]{1,0:T(4,128)S(1)}, f32[4,1280]{1,0:T(4,128)S(1)}, u32[]{:S(2)}, u32[]{:S(2)}) collective-permute-start(f32[4,1280]{1,0:T(4,128)S(1)} %fusion.14.after_ref), channel_id=1, source_target_pairs={{0,1},{1,0},{2,3},{3,2},{4,5},{5,4},{6,7},{7,6},{8,9},{9,8},{10,11... | collective-permute-start | bytes 61448 | tf_op jit(solution)/shard_map/ppermute | solution.py:214
  44.3 1.3 %collective-permute-start.2 = (f32[4,1280]{1,0:T(4,128)S(1)}, f32[4,1280]{1,0:T(4,128)S(1)}, u32[]{:S(2)}, u32[]{:S(2)}) collective-permute-start(f32[4,1280]{1,0:T(4,128)S(1)} %slice_select_fusion.after_ref), channel_id=1, source_target_pairs={{0,1},{1,0},{2,3},{3,2},{4,5},{5,4},{6,7},{7,6},{8,9},{9,8},{10,11... | collective-permute-start | bytes 61448 | tf_op jit(solution)/shard_map/ppermute | solution.py:214
  68.6 3.6 %collective-permute-start.3 = (f32[4,1280]{1,0:T(4,128)S(1)}, f32[4,1280]{1,0:T(4,128)S(1)}, u32[]{:S(2)}, u32[]{:S(2)}) collective-permute-start(f32[4,1280]{1,0:T(4,128)S(1)} %fusion.2.after_ref), channel_id=1, source_target_pairs={{0,1},{1,0},{2,3},{3,2},{4,5},{5,4},{6,7},{7,6},{8,9},{9,8},{10,11... | collective-permute-start | bytes 61448 | tf_op jit(solution)/shard_map/ppermute | solution.py:214

commit v3 on v2

--- a/solution.py
+++ b/solution.py
@@ -1,4 +1,5 @@
 import functools
+import math
 
 import jax
 import jax.numpy as jnp
@@ -138,7 +139,9 @@
     if block is not None:
         m_ref[...] = merged_rows(block, a_ref, g_ref, e_ref)
     hat = orthonormal(p_ref[...])
-    hat_ref[...] = hat
+    p1, p2, p3 = parts_of(hat)
+    zero = jnp.zeros_like(hat)
+    hat_ref[...] = jnp.concatenate([p1, p1, p2, p2, p1, p3, zero, zero], axis=0).astype(BF16).T
     stack = stacked(hat)
     left = stacked(times(stack, a_ref[...], NT))
     q_ref[...] = times(stack, e_ref[...], NN) + times(left, g_ref[...], NN)
@@ -149,7 +152,7 @@
         functools.partial(q_kernel, block=block),
         out_shape=(
             jax.ShapeDtypeStruct(p_sum.shape, F32),
-            pltpu.VMEM(p_sum.shape, F32),
+            pltpu.VMEM((p_sum.shape[1], 8 * p_sum.shape[0]), BF16),
             pltpu.VMEM((BLOCK, e.shape[1]), F32),
         ),
         in_specs=[VMEM, VMEM, VMEM, VMEM],
@@ -166,14 +169,13 @@
     f_ref[...] = factor
     copies = [pltpu.make_async_copy(f_ref, f_hbm, sems.at[n])]
     copies[0].start()
-    p1, p2, p3 = parts_of(hat_ref[...])
     f1, f2, f3 = parts_of(factor)
-    zero = jnp.zeros_like(p1)
-    lhs = jnp.concatenate([p1, p1, p2, p2, p1, p3, zero, zero], axis=0).astype(BF16)
+    zero = jnp.zeros_like(f1)
+    lhs = hat_ref[...]
     rhs = jnp.concatenate([f1, f2, f1, f2, f3, f1, zero, zero], axis=0).astype(BF16)
     for i in range(n):
         at = slice(i * BLOCK, (i + 1) * BLOCK)
-        update = lax.dot_general(lhs[:, at], rhs, TN, preferred_element_type=F32)
+        update = lax.dot_general(lhs[at, :], rhs, NN, preferred_element_type=F32)
         out_ref[at, :] = (m_refs[i][...] - update).astype(BF16)
         copies.append(pltpu.make_async_copy(out_ref.at[at], out_hbm.at[at], sems.at[i]))
         copies[-1].start()
@@ -238,11 +240,16 @@
     return jnp.concatenate(rows, axis=0), extra
 
 
-def xy_groups(step):
+def listed(i, step, n):
+    side = math.isqrt(n)
+    return i % side * side + i // side if step == 0 else i * step % n
+
+
+def xy_groups(steps):
     n_row, n_col = lax.axis_size("row"), lax.axis_size("col")
     n = n_col // CORES
     return [
-        [r * n_col + i * step % n * CORES + k for i in range(n)]
+        [r * n_col + listed(i, steps[k], n) * CORES + k for i in range(n)]
         for r in range(n_row)
         for k in range(CORES)
     ]
@@ -259,11 +266,11 @@
     p, a, g, e = p_local(start_q, activations, out_grads, error_buffer)
     block = lambda i: lambda after: merged_block(i, a, g, e, after)
     p, m0 = core_scatter(p, core, block(0))
-    p = gather_sum(gather_sum(p, xy_groups(7)), z_groups([1, 2, 0, 7, 6, 3, 5, 4]))
+    p = gather_sum(gather_sum(p, xy_groups((9, 9))), z_groups([1, 5, 6, 4, 2, 7, 0, 3]))
     p_sum, m1 = core_gather(p, core, block(1))
     q, hat, m2 = q_local(p_sum, a, g, e, 2)
     q, m3 = core_scatter(q, core, block(3))
-    q = gather_sum(gather_sum(q, xy_groups(1)), z_groups([1, 2, 0, 7, 6, 3, 5, 4]))
+    q = gather_sum(gather_sum(q, xy_groups((0, 1))), z_groups([1, 2, 0, 7, 6, 3, 5, 4]))
     q_total, m4 = core_gather(q, core, block(4))
     return update(q_total, hat, [m0, m1, m2, m3, m4], replicas)
 

time: 74.6 us -> 74 us (level)
  no operation moved by 1% of the time
where the time goes in v3:
time: 74 us; the launch traced here: 73.8 us
  blocking collectives  50.2 us (68%)
  Pallas kernels  12.8 us (17%)
  starting transfers between devices  9.51 us (13%)
  between operations  0.8 us (1%)
    all_to_all x4, blocking collectives, gather_sum(): lax.all_to_all(every, AXES, 0, 0, axis_index_groups=groups, tiled=True)  50.2 us
    ppermute x4, starting transfers between devices, permute(): return lax.ppermute(x, AXES, pairs)  9.51 us
    pallas_call x1, Pallas kernels, p_local(): pl.pallas_call(functools.partial(p_kernel, cuts=cuts), out_shape=(jax.Sha...  4.44 us
    pallas_call x4, Pallas kernels, merged_block(): pl.pallas_call(kernel, out_shape=pltpu.VMEM((BLOCK, e.shape[1]), F32), in...  3.56 us
    pallas_call x1, Pallas kernels, q_local(): pl.pallas_call(functools.partial(q_kernel, block=block), out_shape=(jax.S...  2.75 us
    pallas_call x1, Pallas kernels, update(): pl.pallas_call(functools.partial(update_kernel, replicas=replicas, n=n),...  2.06 us
  transfers between devices with their start and end apart: 4, of which 0 were waited for; matrix products, arithmetic and copies ran while one was open for 0% of the time, Pallas kernels for 5%

profile of v3, /device:TPU:1, one launch (start us, length us, event | category | flops | bytes accessed | tf_op | source)
XLA Modules:
  0.0 73.8 jit_solution(15601125728808956052)
XLA Ops:
  0.6 4.4 %p_local.1 = (f32[8,1280]{1,0:T(8,128)S(1)}, bf16[1024,1280]{1,0:T(8,128)(2,1)S(1)}, bf16[1024,1280]{1,0:T(8,128)(2,1)S(1)}, bf16[1280,1280]{1,0:T(8,128)(2,1)S(1)}) custom-call(f32[8,1280]{1,0:T(8,128)} %q_hbm.1, bf16[1024,1280]{1,0:T(8,128)(2,1)} %a_hbm.1, bf16[1024,1280]{1,0:T(8,128)(2,1)} %g_hbm.1, bf16[1280,1280]{1,0:T(8,128)(2,1)} %e_hbm.1), custom_call_target="tpu_custom_call" | custom-call | tf_op jit(solution)/shard_map/p_local/pallas_call | solution.py:86
  5.1 3.3 %collective-permute-start = (f32[4,1280]{1,0:T(4,128)S(1)}, f32[4,1280]{1,0:T(4,128)S(1)}, u32[]{:S(2)}, u32[]{:S(2)}) collective-permute-start(f32[4,1280]{1,0:T(4,128)S(1)} %slice_select_fusion.1.after_ref), channel_id=1, source_target_pairs={{0,1},{1,0},{2,3},{3,2},{4,5},{5,4},{6,7},{7,6},{8,9},{9,8},{10,11... | collective-permute-start | bytes 61448 | tf_op jit(solution)/shard_map/ppermute | solution.py:216
  8.4 0.9 %merged_block.4.refs_0_ = f32[256,1280]{1,0:T(8,128)S(1)} custom-call(bf16[1024,1280]{1,0:T(8,128)(2,1)S(1)} %get-tuple-element.18.a_ref, bf16[1024,1280]{1,0:T(8,128)(2,1)S(1)} %get-tuple-element.19.g_ref, bf16[1280,1280]{1,0:T(8,128)(2,1)S(1)} %get-tuple-element.20.e_ref, f32[4,1280]{1,0:T(4,128)S(1)} %slice_select_fusion.1.after_ref), custom_call_target="tpu_custom_call" | custom-call | flops 671088640 | tf_op jit(solution)/shard_map/merged_block/pallas_call | solution.py:113
  9.3 0.0 collective-permute-done
  9.4 13.8 %all_to_all.20 = f32[16,4,1280]{2,1,0:T(4,128)S(1)} all-to-all(f32[16,4,1280]{2,1,0:T(4,128)S(1)} %broadcast_in_dim.12), channel_id=1, replica_groups={{0,18,4,22,8,26,12,30,16,2,20,6,24,10,28,14},{1,19,5,23,9,27,13,31,17,3..., dimensions={0} | all-to-all | bytes 655360 | tf_op jit(solution)/shard_map/all_to_all | solution.py:222
  23.3 15.2 %all_to_all.21 = f32[8,4,1280]{2,1,0:T(4,128)S(1)} all-to-all(f32[8,4,1280]{2,1,0:T(4,128)S(1)} %broadcast_in_dim.14), channel_id=1, replica_groups={{32,160,192,128,64,224,0,96},{33,161,193,129,65,225,1,97},{34,162,194,1..., dimensions={0} | all-to-all | bytes 327680 | tf_op jit(solution)/shard_map/all_to_all | solution.py:222
  38.5 2.8 %collective-permute-start.1 = (f32[4,1280]{1,0:T(4,128)S(1)}, f32[4,1280]{1,0:T(4,128)S(1)}, u32[]{:S(2)}, u32[]{:S(2)}) collective-permute-start(f32[4,1280]{1,0:T(4,128)S(1)} %fusion.14.after_ref), channel_id=1, source_target_pairs={{0,1},{1,0},{2,3},{3,2},{4,5},{5,4},{6,7},{7,6},{8,9},{9,8},{10,11... | collective-permute-start | bytes 61448 | tf_op jit(solution)/shard_map/ppermute | solution.py:216
  41.3 0.9 %merged_block.5.refs_1_ = f32[256,1280]{1,0:T(8,128)S(1)} custom-call(bf16[1024,1280]{1,0:T(8,128)(2,1)S(1)} %get-tuple-element.18.a_ref, bf16[1024,1280]{1,0:T(8,128)(2,1)S(1)} %get-tuple-element.19.g_ref, bf16[1280,1280]{1,0:T(8,128)(2,1)S(1)} %get-tuple-element.20.e_ref, f32[4,1280]{1,0:T(4,128)S(1)} %fusion.14.after_ref), custom_call_target="tpu_custom_call" | custom-call | flops 671088640 | tf_op jit(solution)/shard_map/merged_block/pallas_call | solution.py:113
  42.2 0.0 collective-permute-done.1
  42.3 2.7 %q_local.1 = (f32[8,1280]{1,0:T(8,128)S(1)}, bf16[1280,64]{1,0:T(8,128)(2,1)S(1)}, f32[256,1280]{1,0:T(8,128)S(1)}) custom-call(f32[8,1280]{1,0:T(8,128)S(1)} %pad_maximum_fusion.p_ref, bf16[1024,1280]{1,0:T(8,128)(2,1)S(1)} %get-tuple-element.18.a_ref, bf16[1024,1280]{1,0:T(8,128)(2,1)S(1)} %get-tuple-element.19.g_ref, ...), custom_call_target="tpu_custom_call" | custom-call | tf_op jit(solution)/shard_map/q_local/pallas_call | solution.py:151
  45.1 0.4 collective-permute-start.2
  45.4 0.9 %merged_block.6.refs_3_ = f32[256,1280]{1,0:T(8,128)S(1)} custom-call(bf16[1024,1280]{1,0:T(8,128)(2,1)S(1)} %get-tuple-element.18.a_ref, bf16[1024,1280]{1,0:T(8,128)(2,1)S(1)} %get-tuple-element.19.g_ref, bf16[1280,1280]{1,0:T(8,128)(2,1)S(1)} %get-tuple-element.20.e_ref, f32[4,1280]{1,0:T(4,128)S(1)} %slice_select_fusion.after_ref), custom_call_target="tpu_custom_call" | custom-call | flops 671088640 | tf_op jit(solution)/shard_map/merged_block/pallas_call | solution.py:113
  46.3 0.0 collective-permute-done.2
  46.4 11.6 %all_to_all.22 = f32[16,4,1280]{2,1,0:T(4,128)S(1)} all-to-all(f32[16,4,1280]{2,1,0:T(4,128)S(1)} %broadcast_in_dim.15), channel_id=1, replica_groups={{0,8,16,24,2,10,18,26,4,12,20,28,6,14,22,30},{1,3,5,7,9,11,13,15,17,19,..., dimensions={0} | all-to-all | bytes 655360 | tf_op jit(solution)/shard_map/all_to_all | solution.py:222
  58.1 9.6 %all_to_all.23 = f32[8,4,1280]{2,1,0:T(4,128)S(1)} all-to-all(f32[8,4,1280]{2,1,0:T(4,128)S(1)} %broadcast_in_dim.33), channel_id=1, replica_groups={{32,64,0,224,192,96,160,128},{33,65,1,225,193,97,161,129},{34,66,2,226,..., dimensions={0} | all-to-all | bytes 327680 | tf_op jit(solution)/shard_map/all_to_all | solution.py:222
  67.7 3.0 %collective-permute-start.3 = (f32[4,1280]{1,0:T(4,128)S(1)}, f32[4,1280]{1,0:T(4,128)S(1)}, u32[]{:S(2)}, u32[]{:S(2)}) collective-permute-start(f32[4,1280]{1,0:T(4,128)S(1)} %fusion.2.after_ref), channel_id=1, source_target_pairs={{0,1},{1,0},{2,3},{3,2},{4,5},{5,4},{6,7},{7,6},{8,9},{9,8},{10,11... | collective-permute-start | bytes 61448 | tf_op jit(solution)/shard_map/ppermute | solution.py:216
  70.7 0.9 %merged_block.7.refs_4_ = f32[256,1280]{1,0:T(8,128)S(1)} custom-call(bf16[1024,1280]{1,0:T(8,128)(2,1)S(1)} %get-tuple-element.18.a_ref, bf16[1024,1280]{1,0:T(8,128)(2,1)S(1)} %get-tuple-element.19.g_ref, bf16[1280,1280]{1,0:T(8,128)(2,1)S(1)} %get-tuple-element.20.e_ref, f32[4,1280]{1,0:T(4,128)S(1)} %fusion.2.after_ref), custom_call_target="tpu_custom_call" | custom-call | flops 671088640 | tf_op jit(solution)/shard_map/merged_block/pallas_call | solution.py:113
  71.6 0.0 collective-permute-done.3
  71.7 2.1 %update.1 = (bf16[1280,1280]{1,0:T(8,128)(2,1)}, f32[8,1280]{1,0:T(8,128)}) custom-call(f32[8,1280]{1,0:T(8,128)S(1)} %pad_maximum_fusion.1.total_ref, bf16[1280,64]{1,0:T(8,128)(2,1)S(1)} %get-tuple-element.26.hat_ref, f32[256,1280]{1,0:T(8,128)S(1)} %merged_block.4.refs_0_, f32[256,1280]{1,0:T(8,128)S(1)} %merged_block.5.refs_1_, ...), custom_call_target="tpu_custom_call" | custom-call | tf_op jit(solution)/shard_map/update/pallas_call | solution.py:189
  (16 shorter events, 0.4 us)
Async XLA Ops:
  5.1 4.2 %collective-permute-start = (f32[4,1280]{1,0:T(4,128)S(1)}, f32[4,1280]{1,0:T(4,128)S(1)}, u32[]{:S(2)}, u32[]{:S(2)}) collective-permute-start(f32[4,1280]{1,0:T(4,128)S(1)} %slice_select_fusion.1.after_ref), channel_id=1, source_target_pairs={{0,1},{1,0},{2,3},{3,2},{4,5},{5,4},{6,7},{7,6},{8,9},{9,8},{10,11... | collective-permute-start | bytes 61448 | tf_op jit(solution)/shard_map/ppermute | solution.py:216
  38.5 3.7 %collective-permute-start.1 = (f32[4,1280]{1,0:T(4,128)S(1)}, f32[4,1280]{1,0:T(4,128)S(1)}, u32[]{:S(2)}, u32[]{:S(2)}) collective-permute-start(f32[4,1280]{1,0:T(4,128)S(1)} %fusion.14.after_ref), channel_id=1, source_target_pairs={{0,1},{1,0},{2,3},{3,2},{4,5},{5,4},{6,7},{7,6},{8,9},{9,8},{10,11... | collective-permute-start | bytes 61448 | tf_op jit(solution)/shard_map/ppermute | solution.py:216
  45.1 1.3 %collective-permute-start.2 = (f32[4,1280]{1,0:T(4,128)S(1)}, f32[4,1280]{1,0:T(4,128)S(1)}, u32[]{:S(2)}, u32[]{:S(2)}) collective-permute-start(f32[4,1280]{1,0:T(4,128)S(1)} %slice_select_fusion.after_ref), channel_id=1, source_target_pairs={{0,1},{1,0},{2,3},{3,2},{4,5},{5,4},{6,7},{7,6},{8,9},{9,8},{10,11... | collective-permute-start | bytes 61448 | tf_op jit(solution)/shard_map/ppermute | solution.py:216
  67.7 3.9 %collective-permute-start.3 = (f32[4,1280]{1,0:T(4,128)S(1)}, f32[4,1280]{1,0:T(4,128)S(1)}, u32[]{:S(2)}, u32[]{:S(2)}) collective-permute-start(f32[4,1280]{1,0:T(4,128)S(1)} %fusion.2.after_ref), channel_id=1, source_target_pairs={{0,1},{1,0},{2,3},{3,2},{4,5},{5,4},{6,7},{7,6},{8,9},{9,8},{10,11... | collective-permute-start | bytes 61448 | tf_op jit(solution)/shard_map/ppermute | solution.py:216

commit v4 on v3

--- a/solution.py
+++ b/solution.py
@@ -9,7 +9,7 @@
 from jax.sharding import PartitionSpec as P
 
 F32, BF16 = jnp.float32, jnp.bfloat16
-BLOCK = 256
+CUTS = (0, 256, 640, 896, 1280)
 VMEM = pl.BlockSpec(memory_space=pltpu.VMEM)
 ANY = pl.BlockSpec(memory_space=pl.ANY)
 HBM = pl.BlockSpec(memory_space=pltpu.HBM)
@@ -99,64 +99,94 @@
     )(in_hbm(start_q), in_hbm(activations), in_hbm(out_grads), in_hbm(error_buffer))
 
 
-def merged_rows(i, a_ref, g_ref, e_ref):
-    at = slice(i * BLOCK, (i + 1) * BLOCK)
+def merged_rows(rows, a_ref, g_ref, e_ref):
+    at = slice(*rows)
     product = lax.dot_general(a_ref[:, at], g_ref[...], TN, preferred_element_type=F32)
     return product + e_ref[at, :].astype(F32)
 
 
-def merged_block(i, a, g, e, after):
+def merged_block(rows, a, g, e, after):
     def kernel(a_ref, g_ref, e_ref, after_ref, m_ref):
         del after_ref
-        m_ref[...] = merged_rows(i, a_ref, g_ref, e_ref)
+        m_ref[...] = merged_rows(rows, a_ref, g_ref, e_ref)
 
     return pl.pallas_call(
         kernel,
-        out_shape=pltpu.VMEM((BLOCK, e.shape[1]), F32),
+        out_shape=pltpu.VMEM((rows[1] - rows[0], e.shape[1]), F32),
         in_specs=[VMEM, VMEM, VMEM, ANY],
         out_specs=VMEM,
         compiler_params=params(),
         cost_estimate=pl.CostEstimate(
-            flops=2 * a.shape[0] * BLOCK * g.shape[1], bytes_accessed=0, transcendentals=0
+            flops=2 * a.shape[0] * (rows[1] - rows[0]) * g.shape[1], bytes_accessed=0, transcendentals=0
         ),
         name="merged_block",
     )(a, g, e, after)
 
 
-def orthonormal(rest):
-    rows = lax.broadcasted_iota(jnp.int32, (rest.shape[0], 1), 0)
+def block_on_core(which, rows, a, g, e, after, before=None):
+    carried = [] if before is None else [in_vmem(before)]
+
+    def kernel(a_ref, g_ref, e_ref, after_ref, *refs):
+        del after_ref
+
+        @pl.when(lax.axis_index("col") % CORES == which)
+        def _():
+            refs[-1][...] = merged_rows(rows, a_ref, g_ref, e_ref)
+
+    return pl.pallas_call(
+        kernel,
+        out_shape=pltpu.VMEM((rows[1] - rows[0], e.shape[1]), F32),
+        in_specs=[VMEM, VMEM, VMEM, ANY] + [VMEM] * len(carried),
+        out_specs=VMEM,
+        input_output_aliases={4: 0} if carried else {},
+        compiler_params=params(),
+        cost_estimate=pl.CostEstimate(
+            flops=2 * a.shape[0] * (rows[1] - rows[0]) * g.shape[1], bytes_accessed=0, transcendentals=0
+        ),
+        name="block_on_core",
+    )(a, g, e, after, *carried)
+
+
+def orthonormal(vectors):
+    n, width = vectors.shape
+    rows = lax.broadcasted_iota(jnp.int32, (n, 128), 0)
+    lanes = lax.broadcasted_iota(jnp.int32, (n, 128), 1)
+    rest = jnp.concatenate([vectors, (rows == lanes).astype(F32)], axis=1)
+    rows = lax.broadcasted_iota(jnp.int32, (n, 1), 0)
     hat = jnp.zeros_like(rest)
-    for j in range(rest.shape[0]):
+    for j in range(n):
         row = rest[j : j + 1]
-        dots = jnp.sum(row * rest, axis=1, keepdims=True)
+        dots = jnp.sum(row[:, :width] * rest[:, :width], axis=1, keepdims=True)
         square = dots[j : j + 1]
         hat = jnp.where(rows == j, row / jnp.sqrt(square), hat)
         rest = rest - (dots / square) * row
-    return hat
-
-
-def q_kernel(p_ref, a_ref, g_ref, e_ref, q_ref, hat_ref, m_ref, *, block):
-    if block is not None:
-        m_ref[...] = merged_rows(block, a_ref, g_ref, e_ref)
-    hat = orthonormal(p_ref[...])
+    return hat[:, :width], hat[:, width:]
+
+
+def q_kernel(p_ref, a_ref, g_ref, e_ref, q_ref, hat_ref):
+    p_sum = p_ref[...]
+    stack = stacked(p_sum)
+    left = stacked(times(stack, a_ref[...], NT))
+    product = times(stack, e_ref[...], NN) + times(left, g_ref[...], NN)
+    hat, factors = orthonormal(p_sum)
     p1, p2, p3 = parts_of(hat)
     zero = jnp.zeros_like(hat)
-    hat_ref[...] = jnp.concatenate([p1, p1, p2, p2, p1, p3, zero, zero], axis=0).astype(BF16).T
-    stack = stacked(hat)
-    left = stacked(times(stack, a_ref[...], NT))
-    q_ref[...] = times(stack, e_ref[...], NN) + times(left, g_ref[...], NN)
-
-
-def q_local(p_sum, a, g, e, block):
-    return pl.pallas_call(
-        functools.partial(q_kernel, block=block),
+    hat_ref[...] = jnp.concatenate([p1, p1, p2, p2, p1, p3, zero, zero], axis=0).astype(BF16)
+    total = factors[:, 0:1] * product[0:1]
+    for j in range(1, p_sum.shape[0]):
+        total = total + factors[:, j : j + 1] * product[j : j + 1]
+    q_ref[...] = total
+
+
+def q_local(p_sum, a, g, e):
+    return pl.pallas_call(
+        q_kernel,
         out_shape=(
             jax.ShapeDtypeStruct(p_sum.shape, F32),
-            pltpu.VMEM((p_sum.shape[1], 8 * p_sum.shape[0]), BF16),
-            pltpu.VMEM((BLOCK, e.shape[1]), F32),
+            pltpu.VMEM((8 * p_sum.shape[0], p_sum.shape[1]), BF16),
         ),
         in_specs=[VMEM, VMEM, VMEM, VMEM],
-        out_specs=(VMEM, VMEM, VMEM),
+        out_specs=(VMEM, VMEM),
         compiler_params=params(),
         name="q_local",
     )(p_sum, a, g, e)
@@ -173,10 +203,12 @@
     zero = jnp.zeros_like(f1)
     lhs = hat_ref[...]
     rhs = jnp.concatenate([f1, f2, f1, f2, f3, f1, zero, zero], axis=0).astype(BF16)
-    for i in range(n):
-        at = slice(i * BLOCK, (i + 1) * BLOCK)
-        update = lax.dot_general(lhs[at, :], rhs, NN, preferred_element_type=F32)
-        out_ref[at, :] = (m_refs[i][...] - update).astype(BF16)
+    start = 0
+    for i, m_ref in enumerate(m_refs):
+        at = slice(start, start + m_ref.shape[0])
+        start = at.stop
+        change = lax.dot_general(lhs[:, at], rhs, TN, preferred_element_type=F32)
+        out_ref[at, :] = (m_ref[...] - change).astype(BF16)
         copies.append(pltpu.make_async_copy(out_ref.at[at], out_hbm.at[at], sems.at[i]))
         copies[-1].start()
     for copy in copies:
@@ -185,7 +217,7 @@
 
 def update(q_total, hat, blocks, replicas):
     n = len(blocks)
-    shape = (n * BLOCK, q_total.shape[1])
+    shape = (sum(block.shape[0] for block in blocks), q_total.shape[1])
     return pl.pallas_call(
         functools.partial(update_kernel, replicas=replicas, n=n),
         out_shape=(
@@ -264,15 +296,22 @@
     replicas = lax.axis_size("row") * lax.axis_size("col")
     core = lax.axis_index("col") & (CORES - 1)
     p, a, g, e = p_local(start_q, activations, out_grads, error_buffer)
-    block = lambda i: lambda after: merged_block(i, a, g, e, after)
-    p, m0 = core_scatter(p, core, block(0))
+    rows = list(zip(CUTS[:-1], CUTS[1:]))
+
+    def gather(x, rows):
+        x, block = lax.optimization_barrier((x, block_on_core(1, rows, a, g, e, x)))
+        return core_gather(
+            x, core, lambda after: block_on_core(0, rows, a, g, e, after, block)
+        )
+
+    p, m0 = core_scatter(p, core, lambda after: merged_block(rows[0], a, g, e, after))
     p = gather_sum(gather_sum(p, xy_groups((9, 9))), z_groups([1, 5, 6, 4, 2, 7, 0, 3]))
-    p_sum, m1 = core_gather(p, core, block(1))
-    q, hat, m2 = q_local(p_sum, a, g, e, 2)
-    q, m3 = core_scatter(q, core, block(3))
+    p_sum, m1 = gather(p, rows[1])
+    q, hat = q_local(p_sum, a, g, e)
+    q, m2 = core_scatter(q, core, lambda after: merged_block(rows[2], a, g, e, after))
     q = gather_sum(gather_sum(q, xy_groups((0, 1))), z_groups([1, 2, 0, 7, 6, 3, 5, 4]))
-    q_total, m4 = core_gather(q, core, block(4))
-    return update(q_total, hat, [m0, m1, m2, m3, m4], replicas)
+    q_total, m3 = gather(q, rows[3])
+    return update(q_total, hat, [m0, m1, m2, m3], replicas)
 
 
 def solution(mesh):

time: 74 us -> 73.4 us (level)
  starting transfers between devices: 9.51 us -> 7.2 us
  waiting for transfers between devices: 0.03 us -> 1.69 us
    ppermute x4, starting transfers between devices: 9.51 us -> 7.2 us  [permute(): return lax.ppermute(x, AXES, pairs)]
    ppermute x4, waiting for transfers between devices: 0.03 us -> 1.69 us  [permute(): return lax.ppermute(x, AXES, pairs)]
    pallas_call x5 -> x7, Pallas kernels: 6.31 us -> 6.25 us  [the longest x4 2.52 us: block_on_core(): pl.pallas_call(kernel, out_shape=pltpu.VMEM((rows[1] - rows[0], e.shape[1...]
  transfers between devices with their start and end apart: 4 -> 4, of which waited for: 0 -> 2; matrix products, arithmetic and copies ran while one was open for 0% -> 0% of each run, Pallas kernels for 5% -> 2%
where the time goes in v4:
time: 73.4 us; the launch traced here: 73.2 us
  blocking collectives  50.3 us (69%)
  Pallas kernels  12.9 us (18%)
  starting transfers between devices  7.2 us (10%)
  waiting for transfers between devices  1.69 us (2%)
  between operations  0.8 us (1%)
    all_to_all x4, blocking collectives, gather_sum(): lax.all_to_all(every, AXES, 0, 0, axis_index_groups=groups, tiled=True)  50.3 us
    ppermute x4, starting transfers between devices, permute(): return lax.ppermute(x, AXES, pairs)  7.2 us
    pallas_call x1, Pallas kernels, p_local(): pl.pallas_call(functools.partial(p_kernel, cuts=cuts), out_shape=(jax.Sha...  4.44 us
    pallas_call x4, Pallas kernels, block_on_core(): pl.pallas_call(kernel, out_shape=pltpu.VMEM((rows[1] - rows[0], e.shape[1...  2.52 us
    pallas_call x1, Pallas kernels, update(): pl.pallas_call(functools.partial(update_kernel, replicas=replicas, n=n),...  2.2 us
    pallas_call x1, Pallas kernels, q_local(): pl.pallas_call(q_kernel, out_shape=(jax.ShapeDtypeStruct(p_sum.shape, F32...  1.94 us
    pallas_call x2, Pallas kernels, merged_block(): pl.pallas_call(kernel, out_shape=pltpu.VMEM((rows[1] - rows[0], e.shape[1...  1.8 us
    ppermute x4, waiting for transfers between devices, permute(): return lax.ppermute(x, AXES, pairs)  1.69 us
  transfers between devices with their start and end apart: 4, of which 2 were waited for; matrix products, arithmetic and copies ran while one was open for 0% of the time, Pallas kernels for 2%

profile of v4, /device:TPU:1, one launch (start us, length us, event | category | flops | bytes accessed | tf_op | source)
XLA Modules:
  0.0 73.2 jit_solution(4954024721940835690)
XLA Ops:
  0.6 4.4 %p_local.1 = (f32[8,1280]{1,0:T(8,128)S(1)}, bf16[1024,1280]{1,0:T(8,128)(2,1)S(1)}, bf16[1024,1280]{1,0:T(8,128)(2,1)S(1)}, bf16[1280,1280]{1,0:T(8,128)(2,1)S(1)}) custom-call(f32[8,1280]{1,0:T(8,128)} %q_hbm.1, bf16[1024,1280]{1,0:T(8,128)(2,1)} %a_hbm.1, bf16[1024,1280]{1,0:T(8,128)(2,1)} %g_hbm.1, bf16[1280,1280]{1,0:T(8,128)(2,1)} %e_hbm.1), custom_call_target="tpu_custom_call" | custom-call | tf_op jit(solution)/shard_map/p_local/pallas_call | solution.py:86
  5.1 3.3 %collective-permute-start = (f32[4,1280]{1,0:T(4,128)S(1)}, f32[4,1280]{1,0:T(4,128)S(1)}, u32[]{:S(2)}, u32[]{:S(2)}) collective-permute-start(f32[4,1280]{1,0:T(4,128)S(1)} %slice_select_fusion.1.after_ref), channel_id=1, source_target_pairs={{0,1},{1,0},{2,3},{3,2},{4,5},{5,4},{6,7},{7,6},{8,9},{9,8},{10,11... | collective-permute-start | bytes 61448 | tf_op jit(solution)/shard_map/ppermute | solution.py:248
  8.4 0.9 %merged_block.2.refs_0_ = f32[256,1280]{1,0:T(8,128)S(1)} custom-call(bf16[1024,1280]{1,0:T(8,128)(2,1)S(1)} %get-tuple-element.21.a_ref, bf16[1024,1280]{1,0:T(8,128)(2,1)S(1)} %get-tuple-element.22.g_ref, bf16[1280,1280]{1,0:T(8,128)(2,1)S(1)} %get-tuple-element.23.e_ref, f32[4,1280]{1,0:T(4,128)S(1)} %slice_select_fusion.1.after_ref), custom_call_target="tpu_custom_call" | custom-call | flops 671088640 | tf_op jit(solution)/shard_map/merged_block/pallas_call | solution.py:113
  9.3 0.0 collective-permute-done
  9.4 13.8 %all_to_all.20 = f32[16,4,1280]{2,1,0:T(4,128)S(1)} all-to-all(f32[16,4,1280]{2,1,0:T(4,128)S(1)} %broadcast_in_dim.12), channel_id=1, replica_groups={{0,18,4,22,8,26,12,30,16,2,20,6,24,10,28,14},{1,19,5,23,9,27,13,31,17,3..., dimensions={0} | all-to-all | bytes 655360 | tf_op jit(solution)/shard_map/all_to_all | solution.py:254
  23.3 15.2 %all_to_all.21 = f32[8,4,1280]{2,1,0:T(4,128)S(1)} all-to-all(f32[8,4,1280]{2,1,0:T(4,128)S(1)} %broadcast_in_dim.14), channel_id=1, replica_groups={{32,160,192,128,64,224,0,96},{33,161,193,129,65,225,1,97},{34,162,194,1..., dimensions={0} | all-to-all | bytes 327680 | tf_op jit(solution)/shard_map/all_to_all | solution.py:254
  38.5 1.3 %block_on_core.4.refs_0_ = f32[384,1280]{1,0:T(8,128)S(1)} custom-call(bf16[1024,1280]{1,0:T(8,128)(2,1)S(1)} %get-tuple-element.21.a_ref, bf16[1024,1280]{1,0:T(8,128)(2,1)S(1)} %get-tuple-element.22.g_ref, bf16[1280,1280]{1,0:T(8,128)(2,1)S(1)} %get-tuple-element.23.e_ref, f32[4,1280]{1,0:T(4,128)S(1)} %fusion.14.after_ref), custom_call_target="tpu_custom_call" | custom-call | flops 1006632960 | tf_op jit(solution)/shard_map/block_on_core/pallas_call | solution.py:136
  39.8 1.6 %collective-permute-start.1 = (f32[4,1280]{1,0:T(4,128)S(1)}, f32[4,1280]{1,0:T(4,128)S(1)}, u32[]{:S(2)}, u32[]{:S(2)}) collective-permute-start(f32[4,1280]{1,0:T(4,128)S(1)} %fusion.14.after_ref), channel_id=1, source_target_pairs={{0,1},{1,0},{2,3},{3,2},{4,5},{5,4},{6,7},{7,6},{8,9},{9,8},{10,11... | collective-permute-start | bytes 61448 | tf_op jit(solution)/shard_map/ppermute | solution.py:248
  41.4 0.8 %collective-permute-done.1 = f32[4,1280]{1,0:T(4,128)S(1)} collective-permute-done((f32[4,1280]{1,0:T(4,128)S(1)}, f32[4,1280]{1,0:T(4,128)S(1)}, u32[]{:S(2)}, u32[]{:S(2)}) %collective-permute-start.1) | collective-permute-done | bytes 20512 | tf_op jit(solution)/shard_map/ppermute | solution.py:248
  42.3 1.9 %q_local.1 = (f32[8,1280]{1,0:T(8,128)S(1)}, bf16[64,1280]{1,0:T(8,128)(2,1)S(1)}) custom-call(f32[8,1280]{1,0:T(8,128)S(1)} %pad_maximum_fusion.p_ref, bf16[1024,1280]{1,0:T(8,128)(2,1)S(1)} %get-tuple-element.21.a_ref, bf16[1024,1280]{1,0:T(8,128)(2,1)S(1)} %get-tuple-element.22.g_ref, bf16[1280,1280]{1,0:T(8,128)(2,1)S(1)} %get-tuple-element.23.e_ref), custom_call_target="tpu_custom_call" | custom-call | tf_op jit(solution)/shard_map/q_local/pallas_call | solution.py:182
  44.2 0.5 collective-permute-start.2
  44.8 0.9 %merged_block.3.refs_2_ = f32[256,1280]{1,0:T(8,128)S(1)} custom-call(bf16[1024,1280]{1,0:T(8,128)(2,1)S(1)} %get-tuple-element.21.a_ref, bf16[1024,1280]{1,0:T(8,128)(2,1)S(1)} %get-tuple-element.22.g_ref, bf16[1280,1280]{1,0:T(8,128)(2,1)S(1)} %get-tuple-element.23.e_ref, f32[4,1280]{1,0:T(4,128)S(1)} %slice_select_fusion.after_ref), custom_call_target="tpu_custom_call" | custom-call | flops 671088640 | tf_op jit(solution)/shard_map/merged_block/pallas_call | solution.py:113
  45.7 0.0 collective-permute-done.2
  45.7 11.6 %all_to_all.22 = f32[16,4,1280]{2,1,0:T(4,128)S(1)} all-to-all(f32[16,4,1280]{2,1,0:T(4,128)S(1)} %broadcast_in_dim.15), channel_id=1, replica_groups={{0,8,16,24,2,10,18,26,4,12,20,28,6,14,22,30},{1,3,5,7,9,11,13,15,17,19,..., dimensions={0} | all-to-all | bytes 655360 | tf_op jit(solution)/shard_map/all_to_all | solution.py:254
  57.4 9.6 %all_to_all.23 = f32[8,4,1280]{2,1,0:T(4,128)S(1)} all-to-all(f32[8,4,1280]{2,1,0:T(4,128)S(1)} %broadcast_in_dim.33), channel_id=1, replica_groups={{32,64,0,224,192,96,160,128},{33,65,1,225,193,97,161,129},{34,66,2,226,..., dimensions={0} | all-to-all | bytes 327680 | tf_op jit(solution)/shard_map/all_to_all | solution.py:254
  67.1 1.3 %block_on_core.6.refs_0_ = f32[384,1280]{1,0:T(8,128)S(1)} custom-call(bf16[1024,1280]{1,0:T(8,128)(2,1)S(1)} %get-tuple-element.21.a_ref, bf16[1024,1280]{1,0:T(8,128)(2,1)S(1)} %get-tuple-element.22.g_ref, bf16[1280,1280]{1,0:T(8,128)(2,1)S(1)} %get-tuple-element.23.e_ref, f32[4,1280]{1,0:T(4,128)S(1)} %fusion.2.after_ref), custom_call_target="tpu_custom_call" | custom-call | flops 1006632960 | tf_op jit(solution)/shard_map/block_on_core/pallas_call | solution.py:136
  68.4 1.8 %collective-permute-start.3 = (f32[4,1280]{1,0:T(4,128)S(1)}, f32[4,1280]{1,0:T(4,128)S(1)}, u32[]{:S(2)}, u32[]{:S(2)}) collective-permute-start(f32[4,1280]{1,0:T(4,128)S(1)} %fusion.2.after_ref), channel_id=1, source_target_pairs={{0,1},{1,0},{2,3},{3,2},{4,5},{5,4},{6,7},{7,6},{8,9},{9,8},{10,11... | collective-permute-start | bytes 61448 | tf_op jit(solution)/shard_map/ppermute | solution.py:248
  70.1 0.8 %collective-permute-done.3 = f32[4,1280]{1,0:T(4,128)S(1)} collective-permute-done((f32[4,1280]{1,0:T(4,128)S(1)}, f32[4,1280]{1,0:T(4,128)S(1)}, u32[]{:S(2)}, u32[]{:S(2)}) %collective-permute-start.3) | collective-permute-done | bytes 20512 | tf_op jit(solution)/shard_map/ppermute | solution.py:248
  71.0 2.2 %update.1 = (bf16[1280,1280]{1,0:T(8,128)(2,1)}, f32[8,1280]{1,0:T(8,128)}) custom-call(f32[8,1280]{1,0:T(8,128)S(1)} %pad_maximum_fusion.1.total_ref, bf16[64,1280]{1,0:T(8,128)(2,1)S(1)} %get-tuple-element.33.hat_ref, f32[256,1280]{1,0:T(8,128)S(1)} %merged_block.2.refs_0_, f32[384,1280]{1,0:T(8,128)S(1)} %block_on_core.5.refs_1_, ...), custom_call_target="tpu_custom_call" | custom-call | tf_op jit(solution)/shard_map/update/pallas_call | solution.py:221
  (18 shorter events, 0.3 us)
Async XLA Ops:
  5.1 4.2 %collective-permute-start = (f32[4,1280]{1,0:T(4,128)S(1)}, f32[4,1280]{1,0:T(4,128)S(1)}, u32[]{:S(2)}, u32[]{:S(2)}) collective-permute-start(f32[4,1280]{1,0:T(4,128)S(1)} %slice_select_fusion.1.after_ref), channel_id=1, source_target_pairs={{0,1},{1,0},{2,3},{3,2},{4,5},{5,4},{6,7},{7,6},{8,9},{9,8},{10,11... | collective-permute-start | bytes 61448 | tf_op jit(solution)/shard_map/ppermute | solution.py:248
  39.8 2.4 %collective-permute-start.1 = (f32[4,1280]{1,0:T(4,128)S(1)}, f32[4,1280]{1,0:T(4,128)S(1)}, u32[]{:S(2)}, u32[]{:S(2)}) collective-permute-start(f32[4,1280]{1,0:T(4,128)S(1)} %fusion.14.after_ref), channel_id=1, source_target_pairs={{0,1},{1,0},{2,3},{3,2},{4,5},{5,4},{6,7},{7,6},{8,9},{9,8},{10,11... | collective-permute-start | bytes 61448 | tf_op jit(solution)/shard_map/ppermute | solution.py:248
  44.2 1.4 %collective-permute-start.2 = (f32[4,1280]{1,0:T(4,128)S(1)}, f32[4,1280]{1,0:T(4,128)S(1)}, u32[]{:S(2)}, u32[]{:S(2)}) collective-permute-start(f32[4,1280]{1,0:T(4,128)S(1)} %slice_select_fusion.after_ref), channel_id=1, source_target_pairs={{0,1},{1,0},{2,3},{3,2},{4,5},{5,4},{6,7},{7,6},{8,9},{9,8},{10,11... | collective-permute-start | bytes 61448 | tf_op jit(solution)/shard_map/ppermute | solution.py:248
  68.4 2.6 %collective-permute-start.3 = (f32[4,1280]{1,0:T(4,128)S(1)}, f32[4,1280]{1,0:T(4,128)S(1)}, u32[]{:S(2)}, u32[]{:S(2)}) collective-permute-start(f32[4,1280]{1,0:T(4,128)S(1)} %fusion.2.after_ref), channel_id=1, source_target_pairs={{0,1},{1,0},{2,3},{3,2},{4,5},{5,4},{6,7},{7,6},{8,9},{9,8},{10,11... | collective-permute-start | bytes 61448 | tf_op jit(solution)/shard_map/ppermute | solution.py:248

commit v5 on v4

--- a/solution.py
+++ b/solution.py
@@ -10,6 +10,7 @@
 
 F32, BF16 = jnp.float32, jnp.bfloat16
 CUTS = (0, 256, 640, 896, 1280)
+PIECE = 128
 VMEM = pl.BlockSpec(memory_space=pltpu.VMEM)
 ANY = pl.BlockSpec(memory_space=pl.ANY)
 HBM = pl.BlockSpec(memory_space=pltpu.HBM)
@@ -171,7 +172,7 @@
     hat, factors = orthonormal(p_sum)
     p1, p2, p3 = parts_of(hat)
     zero = jnp.zeros_like(hat)
-    hat_ref[...] = jnp.concatenate([p1, p1, p2, p2, p1, p3, zero, zero], axis=0).astype(BF16)
+    hat_ref[...] = jnp.concatenate([p1, p1, p2, p2, p1, p3, zero, zero], axis=0).astype(BF16).T
     total = factors[:, 0:1] * product[0:1]
     for j in range(1, p_sum.shape[0]):
         total = total + factors[:, j : j + 1] * product[j : j + 1]
@@ -183,7 +184,7 @@
         q_kernel,
         out_shape=(
             jax.ShapeDtypeStruct(p_sum.shape, F32),
-            pltpu.VMEM((8 * p_sum.shape[0], p_sum.shape[1]), BF16),
+            pltpu.VMEM((p_sum.shape[1], 8 * p_sum.shape[0]), BF16),
         ),
         in_specs=[VMEM, VMEM, VMEM, VMEM],
         out_specs=(VMEM, VMEM),
@@ -197,20 +198,22 @@
     out_hbm, f_hbm, f_ref, out_ref, sems = refs[n:]
     factor = total_ref[...] * (1.0 / replicas)
     f_ref[...] = factor
-    copies = [pltpu.make_async_copy(f_ref, f_hbm, sems.at[n])]
+    copies = [pltpu.make_async_copy(f_ref, f_hbm, sems.at[0])]
     copies[0].start()
     f1, f2, f3 = parts_of(factor)
     zero = jnp.zeros_like(f1)
     lhs = hat_ref[...]
     rhs = jnp.concatenate([f1, f2, f1, f2, f3, f1, zero, zero], axis=0).astype(BF16)
     start = 0
-    for i, m_ref in enumerate(m_refs):
-        at = slice(start, start + m_ref.shape[0])
-        start = at.stop
-        change = lax.dot_general(lhs[:, at], rhs, TN, preferred_element_type=F32)
-        out_ref[at, :] = (m_ref[...] - change).astype(BF16)
-        copies.append(pltpu.make_async_copy(out_ref.at[at], out_hbm.at[at], sems.at[i]))
-        copies[-1].start()
+    for m_ref in m_refs:
+        for offset in range(0, m_ref.shape[0], PIECE):
+            at = slice(start, start + PIECE)
+            start = at.stop
+            change = lax.dot_general(lhs[at, :], rhs, NN, preferred_element_type=F32)
+            out_ref[at, :] = (m_ref[offset : offset + PIECE, :] - change).astype(BF16)
+            sem = sems.at[len(copies)]
+            copies.append(pltpu.make_async_copy(out_ref.at[at], out_hbm.at[at], sem))
+            copies[-1].start()
     for copy in copies:
         copy.wait()
 
@@ -229,7 +232,7 @@
         scratch_shapes=[
             pltpu.VMEM(q_total.shape, F32),
             pltpu.VMEM(shape, BF16),
-            pltpu.SemaphoreType.DMA((n + 1,)),
+            pltpu.SemaphoreType.DMA((shape[0] // PIECE + 1,)),
         ],
         compiler_params=params(),
         name="update",

time: 73.4 us -> 73.2 us (level)
  no operation moved by 1% of the time
where the time goes in v5:
time: 73.2 us; the launch traced here: 73 us
  blocking collectives  50.3 us (69%)
  Pallas kernels  12.7 us (17%)
  starting transfers between devices  7.19 us (10%)
  waiting for transfers between devices  1.69 us (2%)
  between operations  0.8 us (1%)
    all_to_all x4, blocking collectives, gather_sum(): lax.all_to_all(every, AXES, 0, 0, axis_index_groups=groups, tiled=True)  50.3 us
    ppermute x4, starting transfers between devices, permute(): return lax.ppermute(x, AXES, pairs)  7.19 us
    pallas_call x1, Pallas kernels, p_local(): pl.pallas_call(functools.partial(p_kernel, cuts=cuts), out_shape=(jax.Sha...  4.44 us
    pallas_call x4, Pallas kernels, block_on_core(): pl.pallas_call(kernel, out_shape=pltpu.VMEM((rows[1] - rows[0], e.shape[1...  2.52 us
    pallas_call x1, Pallas kernels, update(): pl.pallas_call(functools.partial(update_kernel, replicas=replicas, n=n),...  2.03 us
    pallas_call x1, Pallas kernels, q_local(): pl.pallas_call(q_kernel, out_shape=(jax.ShapeDtypeStruct(p_sum.shape, F32...  1.94 us
    pallas_call x2, Pallas kernels, merged_block(): pl.pallas_call(kernel, out_shape=pltpu.VMEM((rows[1] - rows[0], e.shape[1...  1.8 us
    ppermute x4, waiting for transfers between devices, permute(): return lax.ppermute(x, AXES, pairs)  1.69 us
  transfers between devices with their start and end apart: 4, of which 2 were waited for; matrix products, arithmetic and copies ran while one was open for 0% of the time, Pallas kernels for 2%

profile of v5, /device:TPU:1, one launch (start us, length us, event | category | flops | bytes accessed | tf_op | source)
XLA Modules:
  0.0 73.0 jit_solution(3324541207505049951)
XLA Ops:
  0.6 4.4 %p_local.1 = (f32[8,1280]{1,0:T(8,128)S(1)}, bf16[1024,1280]{1,0:T(8,128)(2,1)S(1)}, bf16[1024,1280]{1,0:T(8,128)(2,1)S(1)}, bf16[1280,1280]{1,0:T(8,128)(2,1)S(1)}) custom-call(f32[8,1280]{1,0:T(8,128)} %q_hbm.1, bf16[1024,1280]{1,0:T(8,128)(2,1)} %a_hbm.1, bf16[1024,1280]{1,0:T(8,128)(2,1)} %g_hbm.1, bf16[1280,1280]{1,0:T(8,128)(2,1)} %e_hbm.1), custom_call_target="tpu_custom_call" | custom-call | tf_op jit(solution)/shard_map/p_local/pallas_call | solution.py:87
  5.1 3.3 %collective-permute-start = (f32[4,1280]{1,0:T(4,128)S(1)}, f32[4,1280]{1,0:T(4,128)S(1)}, u32[]{:S(2)}, u32[]{:S(2)}) collective-permute-start(f32[4,1280]{1,0:T(4,128)S(1)} %slice_select_fusion.1.after_ref), channel_id=1, source_target_pairs={{0,1},{1,0},{2,3},{3,2},{4,5},{5,4},{6,7},{7,6},{8,9},{9,8},{10,11... | collective-permute-start | bytes 61448 | tf_op jit(solution)/shard_map/ppermute | solution.py:251
  8.4 0.9 %merged_block.2.refs_0_ = f32[256,1280]{1,0:T(8,128)S(1)} custom-call(bf16[1024,1280]{1,0:T(8,128)(2,1)S(1)} %get-tuple-element.21.a_ref, bf16[1024,1280]{1,0:T(8,128)(2,1)S(1)} %get-tuple-element.22.g_ref, bf16[1280,1280]{1,0:T(8,128)(2,1)S(1)} %get-tuple-element.23.e_ref, f32[4,1280]{1,0:T(4,128)S(1)} %slice_select_fusion.1.after_ref), custom_call_target="tpu_custom_call" | custom-call | flops 671088640 | tf_op jit(solution)/shard_map/merged_block/pallas_call | solution.py:114
  9.3 0.0 collective-permute-done
  9.4 13.8 %all_to_all.20 = f32[16,4,1280]{2,1,0:T(4,128)S(1)} all-to-all(f32[16,4,1280]{2,1,0:T(4,128)S(1)} %broadcast_in_dim.12), channel_id=1, replica_groups={{0,18,4,22,8,26,12,30,16,2,20,6,24,10,28,14},{1,19,5,23,9,27,13,31,17,3..., dimensions={0} | all-to-all | bytes 655360 | tf_op jit(solution)/shard_map/all_to_all | solution.py:257
  23.3 15.2 %all_to_all.21 = f32[8,4,1280]{2,1,0:T(4,128)S(1)} all-to-all(f32[8,4,1280]{2,1,0:T(4,128)S(1)} %broadcast_in_dim.14), channel_id=1, replica_groups={{32,160,192,128,64,224,0,96},{33,161,193,129,65,225,1,97},{34,162,194,1..., dimensions={0} | all-to-all | bytes 327680 | tf_op jit(solution)/shard_map/all_to_all | solution.py:257
  38.5 1.3 %block_on_core.4.refs_0_ = f32[384,1280]{1,0:T(8,128)S(1)} custom-call(bf16[1024,1280]{1,0:T(8,128)(2,1)S(1)} %get-tuple-element.21.a_ref, bf16[1024,1280]{1,0:T(8,128)(2,1)S(1)} %get-tuple-element.22.g_ref, bf16[1280,1280]{1,0:T(8,128)(2,1)S(1)} %get-tuple-element.23.e_ref, f32[4,1280]{1,0:T(4,128)S(1)} %fusion.14.after_ref), custom_call_target="tpu_custom_call" | custom-call | flops 1006632960 | tf_op jit(solution)/shard_map/block_on_core/pallas_call | solution.py:137
  39.8 1.6 %collective-permute-start.1 = (f32[4,1280]{1,0:T(4,128)S(1)}, f32[4,1280]{1,0:T(4,128)S(1)}, u32[]{:S(2)}, u32[]{:S(2)}) collective-permute-start(f32[4,1280]{1,0:T(4,128)S(1)} %fusion.14.after_ref), channel_id=1, source_target_pairs={{0,1},{1,0},{2,3},{3,2},{4,5},{5,4},{6,7},{7,6},{8,9},{9,8},{10,11... | collective-permute-start | bytes 61448 | tf_op jit(solution)/shard_map/ppermute | solution.py:251
  41.4 0.8 %collective-permute-done.1 = f32[4,1280]{1,0:T(4,128)S(1)} collective-permute-done((f32[4,1280]{1,0:T(4,128)S(1)}, f32[4,1280]{1,0:T(4,128)S(1)}, u32[]{:S(2)}, u32[]{:S(2)}) %collective-permute-start.1) | collective-permute-done | bytes 20512 | tf_op jit(solution)/shard_map/ppermute | solution.py:251
  42.3 1.9 %q_local.1 = (f32[8,1280]{1,0:T(8,128)S(1)}, bf16[1280,64]{1,0:T(8,128)(2,1)S(1)}) custom-call(f32[8,1280]{1,0:T(8,128)S(1)} %pad_maximum_fusion.p_ref, bf16[1024,1280]{1,0:T(8,128)(2,1)S(1)} %get-tuple-element.21.a_ref, bf16[1024,1280]{1,0:T(8,128)(2,1)S(1)} %get-tuple-element.22.g_ref, bf16[1280,1280]{1,0:T(8,128)(2,1)S(1)} %get-tuple-element.23.e_ref), custom_call_target="tpu_custom_call" | custom-call | tf_op jit(solution)/shard_map/q_local/pallas_call | solution.py:183
  44.2 0.5 collective-permute-start.2
  44.7 0.9 %merged_block.3.refs_2_ = f32[256,1280]{1,0:T(8,128)S(1)} custom-call(bf16[1024,1280]{1,0:T(8,128)(2,1)S(1)} %get-tuple-element.21.a_ref, bf16[1024,1280]{1,0:T(8,128)(2,1)S(1)} %get-tuple-element.22.g_ref, bf16[1280,1280]{1,0:T(8,128)(2,1)S(1)} %get-tuple-element.23.e_ref, f32[4,1280]{1,0:T(4,128)S(1)} %slice_select_fusion.after_ref), custom_call_target="tpu_custom_call" | custom-call | flops 671088640 | tf_op jit(solution)/shard_map/merged_block/pallas_call | solution.py:114
  45.7 0.0 collective-permute-done.2
  45.7 11.6 %all_to_all.22 = f32[16,4,1280]{2,1,0:T(4,128)S(1)} all-to-all(f32[16,4,1280]{2,1,0:T(4,128)S(1)} %broadcast_in_dim.15), channel_id=1, replica_groups={{0,8,16,24,2,10,18,26,4,12,20,28,6,14,22,30},{1,3,5,7,9,11,13,15,17,19,..., dimensions={0} | all-to-all | bytes 655360 | tf_op jit(solution)/shard_map/all_to_all | solution.py:257
  57.4 9.6 %all_to_all.23 = f32[8,4,1280]{2,1,0:T(4,128)S(1)} all-to-all(f32[8,4,1280]{2,1,0:T(4,128)S(1)} %broadcast_in_dim.33), channel_id=1, replica_groups={{32,64,0,224,192,96,160,128},{33,65,1,225,193,97,161,129},{34,66,2,226,..., dimensions={0} | all-to-all | bytes 327680 | tf_op jit(solution)/shard_map/all_to_all | solution.py:257
  67.1 1.3 %block_on_core.6.refs_0_ = f32[384,1280]{1,0:T(8,128)S(1)} custom-call(bf16[1024,1280]{1,0:T(8,128)(2,1)S(1)} %get-tuple-element.21.a_ref, bf16[1024,1280]{1,0:T(8,128)(2,1)S(1)} %get-tuple-element.22.g_ref, bf16[1280,1280]{1,0:T(8,128)(2,1)S(1)} %get-tuple-element.23.e_ref, f32[4,1280]{1,0:T(4,128)S(1)} %fusion.2.after_ref), custom_call_target="tpu_custom_call" | custom-call | flops 1006632960 | tf_op jit(solution)/shard_map/block_on_core/pallas_call | solution.py:137
  68.4 1.8 %collective-permute-start.3 = (f32[4,1280]{1,0:T(4,128)S(1)}, f32[4,1280]{1,0:T(4,128)S(1)}, u32[]{:S(2)}, u32[]{:S(2)}) collective-permute-start(f32[4,1280]{1,0:T(4,128)S(1)} %fusion.2.after_ref), channel_id=1, source_target_pairs={{0,1},{1,0},{2,3},{3,2},{4,5},{5,4},{6,7},{7,6},{8,9},{9,8},{10,11... | collective-permute-start | bytes 61448 | tf_op jit(solution)/shard_map/ppermute | solution.py:251
  70.1 0.8 %collective-permute-done.3 = f32[4,1280]{1,0:T(4,128)S(1)} collective-permute-done((f32[4,1280]{1,0:T(4,128)S(1)}, f32[4,1280]{1,0:T(4,128)S(1)}, u32[]{:S(2)}, u32[]{:S(2)}) %collective-permute-start.3) | collective-permute-done | bytes 20512 | tf_op jit(solution)/shard_map/ppermute | solution.py:251
  71.0 2.0 %update.1 = (bf16[1280,1280]{1,0:T(8,128)(2,1)}, f32[8,1280]{1,0:T(8,128)}) custom-call(f32[8,1280]{1,0:T(8,128)S(1)} %pad_maximum_fusion.1.total_ref, bf16[1280,64]{1,0:T(8,128)(2,1)S(1)} %get-tuple-element.33.hat_ref, f32[256,1280]{1,0:T(8,128)S(1)} %merged_block.2.refs_0_, f32[384,1280]{1,0:T(8,128)S(1)} %block_on_core.5.refs_1_, ...), custom_call_target="tpu_custom_call" | custom-call | tf_op jit(solution)/shard_map/update/pallas_call | solution.py:224
  (18 shorter events, 0.3 us)
Async XLA Ops:
  5.1 4.2 %collective-permute-start = (f32[4,1280]{1,0:T(4,128)S(1)}, f32[4,1280]{1,0:T(4,128)S(1)}, u32[]{:S(2)}, u32[]{:S(2)}) collective-permute-start(f32[4,1280]{1,0:T(4,128)S(1)} %slice_select_fusion.1.after_ref), channel_id=1, source_target_pairs={{0,1},{1,0},{2,3},{3,2},{4,5},{5,4},{6,7},{7,6},{8,9},{9,8},{10,11... | collective-permute-start | bytes 61448 | tf_op jit(solution)/shard_map/ppermute | solution.py:251
  39.8 2.4 %collective-permute-start.1 = (f32[4,1280]{1,0:T(4,128)S(1)}, f32[4,1280]{1,0:T(4,128)S(1)}, u32[]{:S(2)}, u32[]{:S(2)}) collective-permute-start(f32[4,1280]{1,0:T(4,128)S(1)} %fusion.14.after_ref), channel_id=1, source_target_pairs={{0,1},{1,0},{2,3},{3,2},{4,5},{5,4},{6,7},{7,6},{8,9},{9,8},{10,11... | collective-permute-start | bytes 61448 | tf_op jit(solution)/shard_map/ppermute | solution.py:251
  44.2 1.4 %collective-permute-start.2 = (f32[4,1280]{1,0:T(4,128)S(1)}, f32[4,1280]{1,0:T(4,128)S(1)}, u32[]{:S(2)}, u32[]{:S(2)}) collective-permute-start(f32[4,1280]{1,0:T(4,128)S(1)} %slice_select_fusion.after_ref), channel_id=1, source_target_pairs={{0,1},{1,0},{2,3},{3,2},{4,5},{5,4},{6,7},{7,6},{8,9},{9,8},{10,11... | collective-permute-start | bytes 61448 | tf_op jit(solution)/shard_map/ppermute | solution.py:251
  68.4 2.6 %collective-permute-start.3 = (f32[4,1280]{1,0:T(4,128)S(1)}, f32[4,1280]{1,0:T(4,128)S(1)}, u32[]{:S(2)}, u32[]{:S(2)}) collective-permute-start(f32[4,1280]{1,0:T(4,128)S(1)} %fusion.2.after_ref), channel_id=1, source_target_pairs={{0,1},{1,0},{2,3},{3,2},{4,5},{5,4},{6,7},{7,6},{8,9},{9,8},{10,11... | collective-permute-start | bytes 61448 | tf_op jit(solution)/shard_map/ppermute | solution.py:251

commit v6 on v5

--- a/solution.py
+++ b/solution.py
@@ -50,13 +50,17 @@
     return out[0:8] + (out[8:16] + out[16:24])
 
 
+def ranges(size, n):
+    blocks = size // 256
+    starts = [256 * -(-blocks * i // n) for i in range(n + 1)]
+    return [pl.ds(low, high - low) for low, high in zip(starts[:-1], starts[1:])]
+
+
 def p_kernel(q_hbm, a_hbm, g_hbm, e_hbm, p_ref, a_ref, g_ref, e_ref, q_ref, sems, *, cuts):
     tokens, width = a_ref.shape
     copies = [pltpu.make_async_copy(q_hbm, q_ref, sems.at[0])]
     for src, dst, n in ((g_hbm, g_ref, cuts[0]), (a_hbm, a_ref, cuts[1]), (e_hbm, e_ref, cuts[2])):
-        size = src.shape[0] // n
-        for i in range(n):
-            rows = pl.ds(i * size, size)
+        for rows in ranges(src.shape[0], n):
             copies.append(pltpu.make_async_copy(src.at[rows], dst.at[rows], sems.at[len(copies)]))
     for copy in copies:
         copy.start()
@@ -76,10 +80,9 @@
         at = slice(i * size, (i + 1) * size)
         term = times(left[:, at], a_ref[at, :], NN)
         total = term if total is None else total + term
-    size = width // cuts[2]
-    for i in range(cuts[2]):
+    for rows in ranges(width, cuts[2]):
         next(queue).wait()
-        at = slice(i * size, (i + 1) * size)
+        at = slice(rows.start, rows.start + rows.size)
         p_ref[:, at] = total[:, at] + times(q, e_ref[at, :], NT)
 
 

time: 73.2 us -> 73.3 us (level)
  no operation moved by 1% of the time
where the time goes in v6:
time: 73.3 us; the launch traced here: 73.1 us
  blocking collectives  50.3 us (69%)
  Pallas kernels  12.8 us (17%)
  starting transfers between devices  7.2 us (10%)
  waiting for transfers between devices  1.69 us (2%)
  between operations  0.8 us (1%)
    all_to_all x4, blocking collectives, gather_sum(): lax.all_to_all(every, AXES, 0, 0, axis_index_groups=groups, tiled=True)  50.3 us
    ppermute x4, starting transfers between devices, permute(): return lax.ppermute(x, AXES, pairs)  7.2 us
    pallas_call x1, Pallas kernels, p_local(): pl.pallas_call(functools.partial(p_kernel, cuts=cuts), out_shape=(jax.Sha...  4.54 us
    pallas_call x4, Pallas kernels, block_on_core(): pl.pallas_call(kernel, out_shape=pltpu.VMEM((rows[1] - rows[0], e.shape[1...  2.51 us
    pallas_call x1, Pallas kernels, update(): pl.pallas_call(functools.partial(update_kernel, replicas=replicas, n=n),...  2.03 us
    pallas_call x1, Pallas kernels, q_local(): pl.pallas_call(q_kernel, out_shape=(jax.ShapeDtypeStruct(p_sum.shape, F32...  1.93 us
    pallas_call x2, Pallas kernels, merged_block(): pl.pallas_call(kernel, out_shape=pltpu.VMEM((rows[1] - rows[0], e.shape[1...  1.8 us
    ppermute x4, waiting for transfers between devices, permute(): return lax.ppermute(x, AXES, pairs)  1.69 us
  transfers between devices with their start and end apart: 4, of which 2 were waited for; matrix products, arithmetic and copies ran while one was open for 0% of the time, Pallas kernels for 2%

profile of v6, /device:TPU:1, one launch (start us, length us, event | category | flops | bytes accessed | tf_op | source)
XLA Modules:
  0.0 73.1 jit_solution(12855650599348323433)
XLA Ops:
  0.6 4.5 %p_local.1 = (f32[8,1280]{1,0:T(8,128)S(1)}, bf16[1024,1280]{1,0:T(8,128)(2,1)S(1)}, bf16[1024,1280]{1,0:T(8,128)(2,1)S(1)}, bf16[1280,1280]{1,0:T(8,128)(2,1)S(1)}) custom-call(f32[8,1280]{1,0:T(8,128)} %q_hbm.1, bf16[1024,1280]{1,0:T(8,128)(2,1)} %a_hbm.1, bf16[1024,1280]{1,0:T(8,128)(2,1)} %g_hbm.1, bf16[1280,1280]{1,0:T(8,128)(2,1)} %e_hbm.1), custom_call_target="tpu_custom_call" | custom-call | tf_op jit(solution)/shard_map/p_local/pallas_call | solution.py:90
  5.2 3.3 %collective-permute-start = (f32[4,1280]{1,0:T(4,128)S(1)}, f32[4,1280]{1,0:T(4,128)S(1)}, u32[]{:S(2)}, u32[]{:S(2)}) collective-permute-start(f32[4,1280]{1,0:T(4,128)S(1)} %slice_select_fusion.1.after_ref), channel_id=1, source_target_pairs={{0,1},{1,0},{2,3},{3,2},{4,5},{5,4},{6,7},{7,6},{8,9},{9,8},{10,11... | collective-permute-start | bytes 61448 | tf_op jit(solution)/shard_map/ppermute | solution.py:254
  8.5 0.9 %merged_block.2.refs_0_ = f32[256,1280]{1,0:T(8,128)S(1)} custom-call(bf16[1024,1280]{1,0:T(8,128)(2,1)S(1)} %get-tuple-element.21.a_ref, bf16[1024,1280]{1,0:T(8,128)(2,1)S(1)} %get-tuple-element.22.g_ref, bf16[1280,1280]{1,0:T(8,128)(2,1)S(1)} %get-tuple-element.23.e_ref, f32[4,1280]{1,0:T(4,128)S(1)} %slice_select_fusion.1.after_ref), custom_call_target="tpu_custom_call" | custom-call | flops 671088640 | tf_op jit(solution)/shard_map/merged_block/pallas_call | solution.py:117
  9.4 0.0 collective-permute-done
  9.5 13.8 %all_to_all.20 = f32[16,4,1280]{2,1,0:T(4,128)S(1)} all-to-all(f32[16,4,1280]{2,1,0:T(4,128)S(1)} %broadcast_in_dim.12), channel_id=1, replica_groups={{0,18,4,22,8,26,12,30,16,2,20,6,24,10,28,14},{1,19,5,23,9,27,13,31,17,3..., dimensions={0} | all-to-all | bytes 655360 | tf_op jit(solution)/shard_map/all_to_all | solution.py:260
  23.4 15.2 %all_to_all.21 = f32[8,4,1280]{2,1,0:T(4,128)S(1)} all-to-all(f32[8,4,1280]{2,1,0:T(4,128)S(1)} %broadcast_in_dim.14), channel_id=1, replica_groups={{32,160,192,128,64,224,0,96},{33,161,193,129,65,225,1,97},{34,162,194,1..., dimensions={0} | all-to-all | bytes 327680 | tf_op jit(solution)/shard_map/all_to_all | solution.py:260
  38.6 1.3 %block_on_core.4.refs_0_ = f32[384,1280]{1,0:T(8,128)S(1)} custom-call(bf16[1024,1280]{1,0:T(8,128)(2,1)S(1)} %get-tuple-element.21.a_ref, bf16[1024,1280]{1,0:T(8,128)(2,1)S(1)} %get-tuple-element.22.g_ref, bf16[1280,1280]{1,0:T(8,128)(2,1)S(1)} %get-tuple-element.23.e_ref, f32[4,1280]{1,0:T(4,128)S(1)} %fusion.14.after_ref), custom_call_target="tpu_custom_call" | custom-call | flops 1006632960 | tf_op jit(solution)/shard_map/block_on_core/pallas_call | solution.py:140
  39.9 1.6 %collective-permute-start.1 = (f32[4,1280]{1,0:T(4,128)S(1)}, f32[4,1280]{1,0:T(4,128)S(1)}, u32[]{:S(2)}, u32[]{:S(2)}) collective-permute-start(f32[4,1280]{1,0:T(4,128)S(1)} %fusion.14.after_ref), channel_id=1, source_target_pairs={{0,1},{1,0},{2,3},{3,2},{4,5},{5,4},{6,7},{7,6},{8,9},{9,8},{10,11... | collective-permute-start | bytes 61448 | tf_op jit(solution)/shard_map/ppermute | solution.py:254
  41.5 0.8 %collective-permute-done.1 = f32[4,1280]{1,0:T(4,128)S(1)} collective-permute-done((f32[4,1280]{1,0:T(4,128)S(1)}, f32[4,1280]{1,0:T(4,128)S(1)}, u32[]{:S(2)}, u32[]{:S(2)}) %collective-permute-start.1) | collective-permute-done | bytes 20512 | tf_op jit(solution)/shard_map/ppermute | solution.py:254
  42.3 1.9 %q_local.1 = (f32[8,1280]{1,0:T(8,128)S(1)}, bf16[1280,64]{1,0:T(8,128)(2,1)S(1)}) custom-call(f32[8,1280]{1,0:T(8,128)S(1)} %pad_maximum_fusion.p_ref, bf16[1024,1280]{1,0:T(8,128)(2,1)S(1)} %get-tuple-element.21.a_ref, bf16[1024,1280]{1,0:T(8,128)(2,1)S(1)} %get-tuple-element.22.g_ref, bf16[1280,1280]{1,0:T(8,128)(2,1)S(1)} %get-tuple-element.23.e_ref), custom_call_target="tpu_custom_call" | custom-call | tf_op jit(solution)/shard_map/q_local/pallas_call | solution.py:186
  44.3 0.5 collective-permute-start.2
  44.8 0.9 %merged_block.3.refs_2_ = f32[256,1280]{1,0:T(8,128)S(1)} custom-call(bf16[1024,1280]{1,0:T(8,128)(2,1)S(1)} %get-tuple-element.21.a_ref, bf16[1024,1280]{1,0:T(8,128)(2,1)S(1)} %get-tuple-element.22.g_ref, bf16[1280,1280]{1,0:T(8,128)(2,1)S(1)} %get-tuple-element.23.e_ref, f32[4,1280]{1,0:T(4,128)S(1)} %slice_select_fusion.after_ref), custom_call_target="tpu_custom_call" | custom-call | flops 671088640 | tf_op jit(solution)/shard_map/merged_block/pallas_call | solution.py:117
  45.8 0.0 collective-permute-done.2
  45.8 11.6 %all_to_all.22 = f32[16,4,1280]{2,1,0:T(4,128)S(1)} all-to-all(f32[16,4,1280]{2,1,0:T(4,128)S(1)} %broadcast_in_dim.15), channel_id=1, replica_groups={{0,8,16,24,2,10,18,26,4,12,20,28,6,14,22,30},{1,3,5,7,9,11,13,15,17,19,..., dimensions={0} | all-to-all | bytes 655360 | tf_op jit(solution)/shard_map/all_to_all | solution.py:260
  57.5 9.6 %all_to_all.23 = f32[8,4,1280]{2,1,0:T(4,128)S(1)} all-to-all(f32[8,4,1280]{2,1,0:T(4,128)S(1)} %broadcast_in_dim.33), channel_id=1, replica_groups={{32,64,0,224,192,96,160,128},{33,65,1,225,193,97,161,129},{34,66,2,226,..., dimensions={0} | all-to-all | bytes 327680 | tf_op jit(solution)/shard_map/all_to_all | solution.py:260
  67.2 1.3 %block_on_core.6.refs_0_ = f32[384,1280]{1,0:T(8,128)S(1)} custom-call(bf16[1024,1280]{1,0:T(8,128)(2,1)S(1)} %get-tuple-element.21.a_ref, bf16[1024,1280]{1,0:T(8,128)(2,1)S(1)} %get-tuple-element.22.g_ref, bf16[1280,1280]{1,0:T(8,128)(2,1)S(1)} %get-tuple-element.23.e_ref, f32[4,1280]{1,0:T(4,128)S(1)} %fusion.2.after_ref), custom_call_target="tpu_custom_call" | custom-call | flops 1006632960 | tf_op jit(solution)/shard_map/block_on_core/pallas_call | solution.py:140
  68.4 1.8 %collective-permute-start.3 = (f32[4,1280]{1,0:T(4,128)S(1)}, f32[4,1280]{1,0:T(4,128)S(1)}, u32[]{:S(2)}, u32[]{:S(2)}) collective-permute-start(f32[4,1280]{1,0:T(4,128)S(1)} %fusion.2.after_ref), channel_id=1, source_target_pairs={{0,1},{1,0},{2,3},{3,2},{4,5},{5,4},{6,7},{7,6},{8,9},{9,8},{10,11... | collective-permute-start | bytes 61448 | tf_op jit(solution)/shard_map/ppermute | solution.py:254
  70.2 0.8 %collective-permute-done.3 = f32[4,1280]{1,0:T(4,128)S(1)} collective-permute-done((f32[4,1280]{1,0:T(4,128)S(1)}, f32[4,1280]{1,0:T(4,128)S(1)}, u32[]{:S(2)}, u32[]{:S(2)}) %collective-permute-start.3) | collective-permute-done | bytes 20512 | tf_op jit(solution)/shard_map/ppermute | solution.py:254
  71.1 2.0 %update.1 = (bf16[1280,1280]{1,0:T(8,128)(2,1)}, f32[8,1280]{1,0:T(8,128)}) custom-call(f32[8,1280]{1,0:T(8,128)S(1)} %pad_maximum_fusion.1.total_ref, bf16[1280,64]{1,0:T(8,128)(2,1)S(1)} %get-tuple-element.33.hat_ref, f32[256,1280]{1,0:T(8,128)S(1)} %merged_block.2.refs_0_, f32[384,1280]{1,0:T(8,128)S(1)} %block_on_core.5.refs_1_, ...), custom_call_target="tpu_custom_call" | custom-call | tf_op jit(solution)/shard_map/update/pallas_call | solution.py:227
  (18 shorter events, 0.3 us)
Async XLA Ops:
  5.2 4.2 %collective-permute-start = (f32[4,1280]{1,0:T(4,128)S(1)}, f32[4,1280]{1,0:T(4,128)S(1)}, u32[]{:S(2)}, u32[]{:S(2)}) collective-permute-start(f32[4,1280]{1,0:T(4,128)S(1)} %slice_select_fusion.1.after_ref), channel_id=1, source_target_pairs={{0,1},{1,0},{2,3},{3,2},{4,5},{5,4},{6,7},{7,6},{8,9},{9,8},{10,11... | collective-permute-start | bytes 61448 | tf_op jit(solution)/shard_map/ppermute | solution.py:254
  39.9 2.4 %collective-permute-start.1 = (f32[4,1280]{1,0:T(4,128)S(1)}, f32[4,1280]{1,0:T(4,128)S(1)}, u32[]{:S(2)}, u32[]{:S(2)}) collective-permute-start(f32[4,1280]{1,0:T(4,128)S(1)} %fusion.14.after_ref), channel_id=1, source_target_pairs={{0,1},{1,0},{2,3},{3,2},{4,5},{5,4},{6,7},{7,6},{8,9},{9,8},{10,11... | collective-permute-start | bytes 61448 | tf_op jit(solution)/shard_map/ppermute | solution.py:254
  44.3 1.5 %collective-permute-start.2 = (f32[4,1280]{1,0:T(4,128)S(1)}, f32[4,1280]{1,0:T(4,128)S(1)}, u32[]{:S(2)}, u32[]{:S(2)}) collective-permute-start(f32[4,1280]{1,0:T(4,128)S(1)} %slice_select_fusion.after_ref), channel_id=1, source_target_pairs={{0,1},{1,0},{2,3},{3,2},{4,5},{5,4},{6,7},{7,6},{8,9},{9,8},{10,11... | collective-permute-start | bytes 61448 | tf_op jit(solution)/shard_map/ppermute | solution.py:254
  68.4 2.6 %collective-permute-start.3 = (f32[4,1280]{1,0:T(4,128)S(1)}, f32[4,1280]{1,0:T(4,128)S(1)}, u32[]{:S(2)}, u32[]{:S(2)}) collective-permute-start(f32[4,1280]{1,0:T(4,128)S(1)} %fusion.2.after_ref), channel_id=1, source_target_pairs={{0,1},{1,0},{2,3},{3,2},{4,5},{5,4},{6,7},{7,6},{8,9},{9,8},{10,11... | collective-permute-start | bytes 61448 | tf_op jit(solution)/shard_map/ppermute | solution.py:254
